TPU v7x, 32 devices: a whole 2x2x4 slice. The times are simulated.
32 devices in a mesh: slab: 8 (over y, x, core), pblk: 4 (over z).
Axes of the slice: x: 2, y: 2, z: 4, core: 2. Of those that a mesh axis runs over, the one named last changes fastest.
Arguments:
- gas_field: float32 [3, 512, 4096], P(None, 'slab', 'pblk'), may hold values from -6 to 6
- drift_field: float32 [2, 512, 4096], P(None, 'slab', 'pblk'), may hold values from 0.2 to 1
- particles: float32 [16384, 3, 128], P(('slab', 'pblk')), may hold values from -6 to 6
- coupling_rates: float32 [16384, 2, 128], P(('slab', 'pblk')), may hold values from 0.1 to 2
- block_owner: int32 [16384, 1], P(('slab', 'pblk')), may hold values from 0 to 31; in each aligned block of 512 rows (0 to 511, 512 to 1023, ...) at most 32 rows name the same one
- cell_index: int32 [16384, 128], P(('slab', 'pblk')), may hold values from 0 to 65535, as said below
- block_pairs: int32 [4096, 2], P(('slab', 'pblk')), may hold values from 0 to 511
- contact: int32 [4096, 128, 128], P(('slab', 'pblk')), may hold values 0 or 1
Outputs:
- gas_next: float32 [3, 512, 4096], P(None, 'slab', 'pblk')
- particles_next: float32 [16384, 3, 128], P(('slab', 'pblk'))
Inputs may be any that keep to these rules, and one draw needn't show every extreme that they name: `block_owner`: of the rows of one device, at most 32 name the same owner, a bound that some block reaches. All particles of one block have the same cell_index // 128. `block_pairs`: both entries name blocks among the rows of the device that holds the pair.
All inputs are finite; a program needn't handle non-finite values. No bound on the sum of `contact` on one device may be relied on, other than what follows from the above.
Results may differ from a plain program's by a relative error of at most 0.000088.
Values sent between devices are 32-bit elements; how exact they have to be, the bound alone decides.
A program may use at most 64 MiB of HBM per device.

v0:
```python
import jax
import jax.numpy as jnp
from jax import lax
from jax.sharding import PartitionSpec as P

BLOCK = 128


TIME_STEP = 0.2
VISCOSITY = 0.25
LOADING = 0.5
DAMPING = 0.1
CONDUCTION = 0.1


def padded_2(block, sides, width):
    for axis, dim in sides:
        count = lax.axis_size(axis)
        forward = [(i, i + 1) for i in range(count - 1)]
        backward = [(target, source) for source, target in forward]
        low = lax.ppermute(
            lax.slice_in_dim(block, block.shape[dim] - width, None, axis=dim), axis, forward
        )
        high = lax.ppermute(lax.slice_in_dim(block, 0, width, axis=dim), axis, backward)
        block = jnp.concatenate([low, block, high], axis=dim)
    return block


def tendency(padded, drift_center):
    middle = padded[:, 1:-1, 1:-1]
    west_cell = padded[:, :-2, 1:-1]
    east_cell = padded[:, 2:, 1:-1]
    south_cell = padded[:, 1:-1, :-2]
    north_cell = padded[:, 1:-1, 2:]
    upwind = drift_center[0] * (middle - west_cell) + drift_center[1] * (middle - south_cell)
    spread = west_cell + east_cell + south_cell + north_cell - 4.0 * middle
    return VISCOSITY * spread - upwind


def coupling_terms(gas_values, particle_state, rate_state):
    drag_force = rate_state[0] * (gas_values[0:2] - particle_state[0:2])
    heat_flow = rate_state[1] * (gas_values[2] - particle_state[2])
    return jnp.concatenate([drag_force, heat_flow[None]], axis=0)


def contact_terms(blocks, block_pairs, contact):
    first_block = blocks[block_pairs[:, 0]]
    second_block = blocks[block_pairs[:, 1]]
    weight = contact.astype(jnp.float32)
    into_first = (
        jnp.einsum("pij,pcj->pci", weight, second_block, precision=lax.Precision.HIGHEST)
        - jnp.sum(weight, axis=2)[:, None, :] * first_block
    )
    into_second = (
        jnp.einsum("pij,pci->pcj", weight, first_block, precision=lax.Precision.HIGHEST)
        - jnp.sum(weight, axis=1)[:, None, :] * second_block
    )
    summed = (
        jnp.zeros_like(blocks)
        .at[block_pairs[:, 0]]
        .add(into_first)
        .at[block_pairs[:, 1]]
        .add(into_second)
    )
    factor = jnp.array([DAMPING, DAMPING, CONDUCTION], jnp.float32)
    return summed * factor[None, :, None]


def group_count(total):
    groups = 1
    while groups < 8 and total % (groups * 2) == 0:
        groups = groups * 2
    return groups


def lookup_cells(tile_table, tile_of, offsets, tile_width, groups):
    tile_count = tile_table.shape[1]
    slot_total = tile_of.shape[0]
    selector = (tile_of[:, None] == jnp.arange(tile_count, dtype=jnp.int32)[None, :]).astype(
        jnp.float32
    )
    fetched = jnp.einsum("st,ctq->csq", selector, tile_table, precision=lax.Precision.HIGHEST)
    fetched = jnp.moveaxis(fetched.reshape(3, groups, slot_total // groups, tile_width), 1, 0)
    grouped_offsets = offsets.reshape(groups, slot_total // groups, offsets.shape[1])

    def pick(item):
        matches = item[1][:, :, None] == jnp.arange(tile_width, dtype=jnp.int32)[None, None, :]
        return jnp.sum(jnp.where(matches[None], item[0][:, :, None, :], 0.0), axis=3)

    picked = lax.map(pick, (fetched, grouped_offsets))
    return jnp.moveaxis(picked, 0, 1).reshape(3, slot_total, offsets.shape[1])


def spread_cells(values, tile_of, offsets, tile_count, tile_width, groups):
    slot_total = tile_of.shape[0]
    grouped_values = jnp.moveaxis(
        values.reshape(3, groups, slot_total // groups, offsets.shape[1]), 1, 0
    )
    grouped_offsets = offsets.reshape(groups, slot_total // groups, offsets.shape[1])

    def spread(item):
        matches = item[1][:, :, None] == jnp.arange(tile_width, dtype=jnp.int32)[None, None, :]
        return jnp.sum(jnp.where(matches[None], item[0][:, :, :, None], 0.0), axis=2)

    tile_rows = jnp.moveaxis(lax.map(spread, (grouped_values, grouped_offsets)), 0, 1).reshape(
        3, slot_total, tile_width
    )
    selector = (tile_of[:, None] == jnp.arange(tile_count, dtype=jnp.int32)[None, :]).astype(
        jnp.float32
    )
    return jnp.einsum("st,csq->ctq", selector, tile_rows, precision=lax.Precision.HIGHEST)


def on_device(
    gas_field, drift_field, particles, coupling_rates, block_owner, cell_index, block_pairs, contact
):
    contact_force = jnp.swapaxes(contact_terms(particles, block_pairs, contact), 0, 1)
    padded = padded_2(gas_field, (("slab", 1), ("pblk", 2)), 1)
    section_one = gas_field + TIME_STEP * tendency(padded, drift_field)
    padded_one = padded_2(section_one, (("slab", 1), ("pblk", 2)), 1)
    section_two = 0.5 * (gas_field + section_one + TIME_STEP * tendency(padded_one, drift_field))
    device_count = lax.axis_size("slab") * lax.axis_size("pblk")
    block_count = block_owner.shape[0]
    slot_count = max(2, 2 * block_count // device_count)
    slot_total = device_count * slot_count
    tile_width = min(128, gas_field.shape[2])
    tile_count = gas_field.shape[1] * gas_field.shape[2] // tile_width
    groups = group_count(slot_total)
    target = block_owner[:, 0]
    matches = (target[:, None] == jnp.arange(device_count, dtype=jnp.int32)[None, :]).astype(
        jnp.int32
    )
    position = jnp.sum((jnp.cumsum(matches, axis=0) - matches) * matches, axis=1)
    slot_of = target * slot_count + position
    requests = jnp.zeros((slot_total, BLOCK), jnp.int32).at[slot_of].set(cell_index)
    requests = requests.reshape(device_count, slot_count, BLOCK)
    asked_cells = lax.all_to_all(
        requests, ("slab", "pblk"), split_axis=0, concat_axis=0, tiled=True
    )
    asked_flat = asked_cells.reshape(slot_total, BLOCK)
    tile_of = asked_flat[:, 0] // tile_width
    offsets = asked_flat % tile_width
    tile_table = section_two.reshape(3, tile_count, tile_width)
    local_values = lookup_cells(tile_table, tile_of, offsets, tile_width, groups).reshape(
        3, device_count, slot_count, BLOCK
    )
    particle_state = jnp.swapaxes(particles, 0, 1)
    rate_state = jnp.swapaxes(coupling_rates, 0, 1)
    gas_values = lax.all_to_all(
        local_values, ("slab", "pblk"), split_axis=1, concat_axis=1, tiled=True
    )
    picked = gas_values.reshape(3, slot_total, BLOCK)[:, slot_of]
    exchange_terms = coupling_terms(picked, particle_state, rate_state)
    outgoing = jnp.zeros((3, slot_total, BLOCK), jnp.float32).at[:, slot_of].set(exchange_terms)
    outgoing = outgoing.reshape(3, device_count, slot_count, BLOCK)
    arrived = lax.all_to_all(outgoing, ("slab", "pblk"), split_axis=1, concat_axis=1, tiled=True)
    sources = spread_cells(
        arrived.reshape(3, slot_total, BLOCK), tile_of, offsets, tile_count, tile_width, groups
    )
    gas_next = section_two - TIME_STEP * LOADING * sources.reshape(section_two.shape)
    updated = particle_state + TIME_STEP * (exchange_terms + contact_force)
    return (gas_next, jnp.swapaxes(updated, 0, 1))


def solution(mesh):
    in_specs = (
        P(None, "slab", "pblk"),
        P(None, "slab", "pblk"),
        P(("slab", "pblk"), None, None),
        P(("slab", "pblk"), None, None),
        P(("slab", "pblk"), None),
        P(("slab", "pblk"), None),
        P(("slab", "pblk"), None),
        P(("slab", "pblk"), None, None),
    )
    out_specs = (P(None, "slab", "pblk"), P(("slab", "pblk"), None, None))
    return jax.shard_map(
        on_device, mesh=mesh, in_specs=in_specs, out_specs=out_specs, check_vma=False
    )
```

profile of v0, /device:TPU:1, one launch (start us, length us, event | category | flops | bytes accessed | tf_op | source)
XLA Modules:
  0.0 392.4 jit_solution(3383776510147237630)
XLA Ops:
  1.7 4.5 %collective-permute-start = (f32[3,1,1024]{2,1,0:T(1,128)S(1)}, f32[3,1,1024]{2,1,0:T(1,128)S(1)}, u32[]{:S(2)}, u32[]{:S(2)}) collective-permute-start(f32[3,1,1024]{2,1,0:T(1,128)S(1)} %get-tuple-element.98), channel_id=1, source_target_pairs={{0,4},{4,8},{8,12},{12,16},{16,20},{20,24},{24,28},{1,5},{5,9},{9,... | collective-permute-start | bytes 36872 | tf_op jit(solution)/shard_map/ppermute | solution.py:21
  6.2 1.9 collective-permute-start.1
  11.8 2.9 scatter_custom_fusion
  14.6 6.2 %all-to-all-start = ((s32[32,32,128]{2,1,0:T(8,128)}), s32[32,32,128]{2,1,0:T(8,128)S(1)}, u32[]{:S(2)}, u32[]{:S(2)}) async-start(s32[32,32,128]{2,1,0:T(8,128)} %bitcast.13), calls=%async_computation | async-start | bytes 1048576 | tf_op jit(solution)/shard_map/all_to_all | solution.py:137
  21.0 3.3 collective-permute-start.2
  25.7 6.3 %collective-permute-done.2 = f32[3,66,1]{2,1,0:T(8,128)S(1)} collective-permute-done((f32[3,66,1]{2,1,0:T(8,128)S(1)}, f32[3,66,1]{2,1,0:T(8,128)S(1)}, u32[]{:S(2)}, u32[]{:S(2)}) %collective-permute-start.2) | collective-permute-done | bytes 824 | tf_op jit(solution)/shard_map/ppermute | solution.py:21
  32.7 5.0 %collective-permute-start.4 = (f32[3,1,1024]{2,1,0:T(1,128)S(1)}, f32[3,1,1024]{2,1,0:T(1,128)S(1)}, u32[]{:S(2)}, u32[]{:S(2)}) collective-permute-start(f32[3,1,1024]{2,1,0:T(1,128)S(1)} %get-tuple-element.96), channel_id=1, source_target_pairs={{0,4},{4,8},{8,12},{12,16},{16,20},{20,24},{24,28},{1,5},{5,9},{9,... | collective-permute-start | bytes 36872 | tf_op jit(solution)/shard_map/ppermute | solution.py:21
  37.6 1.9 collective-permute-start.5
  39.6 3.1 collective-permute-done.5
  42.8 6.8 %collective-permute-start.6 = (f32[3,66,1]{2,1,0:T(8,128)S(1)}, f32[3,66,1]{2,1,0:T(8,128)S(1)}, u32[]{:S(2)}, u32[]{:S(2)}) collective-permute-start(f32[3,66,1]{2,1,0:T(8,128)S(1)} %get-tuple-element.90), channel_id=1, source_target_pairs={{0,1},{1,2},{2,3},{4,5},{5,6},{6,7},{8,9},{9,10},{10,11},{12,13},{... | collective-permute-start | bytes 2384 | tf_op jit(solution)/shard_map/ppermute | solution.py:21
  51.3 3.9 collective-permute-done.7
  55.1 1.6 fusion.33
  57.3 2.9 fusion.7
  60.5 1.7 copy.68
  62.6 86.1 %while.20 = (s32[]{:T(128)}, f32[8,3,128,128]{3,2,0,1:T(8,128)S(1)}, s32[8,128,128]{2,1,0:T(8,128)S(1)}, f32[8,3,128,128]{3,2,1,0:T(8,128)}, s32[]{:T(128)}) while((s32[]{:T(128)}, f32[8,3,128,128]{3,2,0,1:T(8,128)S(1)}, s32[8,128,128]{2,1,0:T(8,128)S(1)}, f32[8,3,128,128]{3,2,1,0:T(8,128)}, s32[]{:T(128)}) %tuple.60), condition=%wide.region_6.7_spmd, body=%wide.region_4.6_spmd.sunk | while | flops 14630914 | bytes 5570633 | solution.py:90
  62.6 2.8 iota_compare_fusion.7
  66.3 7.0 %select_reduce_fusion.4 = f32[3,128,128]{2,1,0:T(8,128)S(1)} fusion(f32[3,128,128]{2,1,0:T(8,128)S(1)} %dynamic-slice_bitcast_fusion.8, pred[128,128,128]{2,1,0:T(8,128)(4,1)S(1)} %iota_compare_fusion.7), kind=kLoop, calls=%fused_computation.7.clone.1 | loop fusion | flops 12533760 | bytes 2490368 | tf_op jit(solution)/shard_map/while/body/eval_jaxpr/reduce_sum | solution.py:88
  73.4 2.8 iota_compare_fusion.7
  77.1 7.0 %select_reduce_fusion.4 = f32[3,128,128]{2,1,0:T(8,128)S(1)} fusion(f32[3,128,128]{2,1,0:T(8,128)S(1)} %dynamic-slice_bitcast_fusion.8, pred[128,128,128]{2,1,0:T(8,128)(4,1)S(1)} %iota_compare_fusion.7), kind=kLoop, calls=%fused_computation.7.clone.1 | loop fusion | flops 12533760 | bytes 2490368 | tf_op jit(solution)/shard_map/while/body/eval_jaxpr/reduce_sum | solution.py:88
  84.1 2.8 iota_compare_fusion.7
  87.9 7.0 %select_reduce_fusion.4 = f32[3,128,128]{2,1,0:T(8,128)S(1)} fusion(f32[3,128,128]{2,1,0:T(8,128)S(1)} %dynamic-slice_bitcast_fusion.8, pred[128,128,128]{2,1,0:T(8,128)(4,1)S(1)} %iota_compare_fusion.7), kind=kLoop, calls=%fused_computation.7.clone.1 | loop fusion | flops 12533760 | bytes 2490368 | tf_op jit(solution)/shard_map/while/body/eval_jaxpr/reduce_sum | solution.py:88
  94.9 2.8 iota_compare_fusion.7
  98.6 7.0 %select_reduce_fusion.4 = f32[3,128,128]{2,1,0:T(8,128)S(1)} fusion(f32[3,128,128]{2,1,0:T(8,128)S(1)} %dynamic-slice_bitcast_fusion.8, pred[128,128,128]{2,1,0:T(8,128)(4,1)S(1)} %iota_compare_fusion.7), kind=kLoop, calls=%fused_computation.7.clone.1 | loop fusion | flops 12533760 | bytes 2490368 | tf_op jit(solution)/shard_map/while/body/eval_jaxpr/reduce_sum | solution.py:88
  105.6 2.8 iota_compare_fusion.7
  109.4 7.0 %select_reduce_fusion.4 = f32[3,128,128]{2,1,0:T(8,128)S(1)} fusion(f32[3,128,128]{2,1,0:T(8,128)S(1)} %dynamic-slice_bitcast_fusion.8, pred[128,128,128]{2,1,0:T(8,128)(4,1)S(1)} %iota_compare_fusion.7), kind=kLoop, calls=%fused_computation.7.clone.1 | loop fusion | flops 12533760 | bytes 2490368 | tf_op jit(solution)/shard_map/while/body/eval_jaxpr/reduce_sum | solution.py:88
  116.4 2.8 iota_compare_fusion.7
  120.1 7.0 %select_reduce_fusion.4 = f32[3,128,128]{2,1,0:T(8,128)S(1)} fusion(f32[3,128,128]{2,1,0:T(8,128)S(1)} %dynamic-slice_bitcast_fusion.8, pred[128,128,128]{2,1,0:T(8,128)(4,1)S(1)} %iota_compare_fusion.7), kind=kLoop, calls=%fused_computation.7.clone.1 | loop fusion | flops 12533760 | bytes 2490368 | tf_op jit(solution)/shard_map/while/body/eval_jaxpr/reduce_sum | solution.py:88
  127.2 2.8 iota_compare_fusion.7
  130.9 7.0 %select_reduce_fusion.4 = f32[3,128,128]{2,1,0:T(8,128)S(1)} fusion(f32[3,128,128]{2,1,0:T(8,128)S(1)} %dynamic-slice_bitcast_fusion.8, pred[128,128,128]{2,1,0:T(8,128)(4,1)S(1)} %iota_compare_fusion.7), kind=kLoop, calls=%fused_computation.7.clone.1 | loop fusion | flops 12533760 | bytes 2490368 | tf_op jit(solution)/shard_map/while/body/eval_jaxpr/reduce_sum | solution.py:88
  137.9 2.8 iota_compare_fusion.7
  141.7 7.0 %select_reduce_fusion.4 = f32[3,128,128]{2,1,0:T(8,128)S(1)} fusion(f32[3,128,128]{2,1,0:T(8,128)S(1)} %dynamic-slice_bitcast_fusion.8, pred[128,128,128]{2,1,0:T(8,128)(4,1)S(1)} %iota_compare_fusion.7), kind=kLoop, calls=%fused_computation.7.clone.1 | loop fusion | flops 12533760 | bytes 2490368 | tf_op jit(solution)/shard_map/while/body/eval_jaxpr/reduce_sum | solution.py:88
  150.0 3.5 all-to-all-start.1
  153.6 1.5 copy.109
  156.8 5.7 %convert_reduce_fusion = (f32[128,128]{1,0:T(8,128)S(1)}, f32[128,128]{1,0:T(8,128)S(1)}) fusion(s32[128,128,128]{2,1,0:T(8,128)} %param.20), kind=kLoop, calls=%fused_computation.17 | loop fusion | flops 6258688 | bytes 8519680 | tf_op jit(solution)/shard_map/reduce_sum | solution.py:56
  162.5 15.4 %fusion.15 = f32[128,3,128]{2,1,0:T(4,128)S(1)} fusion(s32[128,128,128]{2,1,0:T(8,128)} %param.20, f32[128,3,128]{2,0,1:T(8,128)S(1)} %gather_fusion.1, f32[128,3,128]{2,0,1:T(8,128)S(1)} %gather_fusion.2, f32[128,128]{1,0:T(8,128)S(1)} %get-tuple-element.73), kind=kOutput, calls=%fused_computation.29 | convolution fusion | flops 77692928 | bytes 9043968 | tf_op jit(solution)/shard_map/pij,pcj->pci/dot_general | solution.py:51
  178.1 4.9 %scatter_fusion.1 = f32[512,3,128]{2,1,0:T(4,128)S(1)} fusion(f32[512,3,128]{2,1,0:T(4,128)S(1)} %broadcast_in_dim.86, s32[128]{0:T(128)S(1)} %get-tuple-element.105, f32[128,3,128]{2,1,0:T(4,128)S(1)} %fusion.15), kind=kCustom, calls=%fused_computation.5 | custom fusion | flops 49152 | bytes 590336 | tf_op jit(solution)/shard_map/scatter-add | solution.py:61
  183.1 9.2 %fusion.18 = f32[128,3,128]{2,1,0:T(4,128)S(1)} fusion(s32[128,128,128]{2,1,0:T(8,128)} %param.20, f32[128,3,128]{2,0,1:T(8,128)S(1)} %gather_fusion.2, f32[128,3,128]{2,0,1:T(8,128)S(1)} %gather_fusion.1, f32[128,128]{1,0:T(8,128)S(1)} %get-tuple-element.72), kind=kOutput, calls=%fused_computation.30 | convolution fusion | flops 77692928 | bytes 9043968 | tf_op jit(solution)/shard_map/pij,pci->pcj/dot_general | solution.py:55
  192.3 4.9 %scatter_fusion.2 = f32[512,3,128]{2,1,0:T(4,128)S(1)} fusion(f32[512,3,128]{2,1,0:T(4,128)S(1)} %scatter_fusion.1, s32[128]{0:T(128)S(1)} %get-tuple-element.104, f32[128,3,128]{2,1,0:T(4,128)S(1)} %fusion.18), kind=kCustom, calls=%fused_computation.6 | custom fusion | flops 49152 | bytes 590336 | tf_op jit(solution)/shard_map/scatter-add | solution.py:63
  197.3 4.1 %copy.71 = f32[3,32,32,128]{3,0,2,1:T(4,128)} copy(f32[3,32,32,128]{3,2,0,1:T(8,128)} %all-to-all-done.1) | data formatting | bytes 3145728 | tf_op jit(solution)/shard_map/all_to_all | solution.py:149
  201.4 4.0 %gather_fusion = f32[512,3,128]{2,1,0:T(4,128)} fusion(f32[3,1024,128]{2,0,1:T(4,128)} %bitcast.127, s32[1024]{0:T(1024)S(1)} %pad_clamp_fusion.2), kind=kCustom, calls=%fused_computation | custom fusion | bytes 1574912 | tf_op jit(solution)/shard_map/gather | solution.py:152
  205.4 2.3 fusion.68
  207.7 1.9 fusion.53
  209.6 2.6 fusion.23
  212.5 31.4 %scatter_fusion = f32[3,1024,128]{2,0,1:T(4,128)S(1)} fusion(f32[3,1024,128]{2,0,1:T(4,128)S(1)} %broadcast_in_dim.85, s32[512]{0:T(512)S(1)} %bitcast.139, f32[512,3,128]{2,1,0:T(4,128)} %get-tuple-element.95), kind=kCustom, calls=%fused_computation.4 | custom fusion | bytes 2361344 | tf_op jit(solution)/shard_map/scatter | solution.py:154
  245.2 5.8 %all-to-all-start.2 = ((f32[3,32,32,128]{3,2,0,1:T(8,128)}), f32[3,32,32,128]{3,2,0,1:T(8,128)S(1)}, u32[]{:S(2)}, u32[]{:S(2)}) async-start(f32[3,32,32,128]{3,2,0,1:T(8,128)} %copy.73), calls=%async_computation.2 | async-start | bytes 3145728 | tf_op jit(solution)/shard_map/all_to_all | solution.py:156
  252.0 36.4 %all-to-all-done.2 = f32[3,32,32,128]{3,2,0,1:T(8,128)S(1)} async-done(((f32[3,32,32,128]{3,2,0,1:T(8,128)}), f32[3,32,32,128]{3,2,0,1:T(8,128)S(1)}, u32[]{:S(2)}, u32[]{:S(2)}) %all-to-all-start.2) | async-done | bytes 1572896 | tf_op jit(solution)/shard_map/all_to_all | solution.py:156
  289.9 99.4 %while.21 = (s32[]{:T(128)}, f32[8,3,128,128]{3,2,0,1:T(8,128)S(1)}, s32[8,128,128]{2,1,0:T(8,128)}, f32[8,3,128,128]{3,2,0,1:T(8,128)}, s32[]{:T(128)}) while((s32[]{:T(128)}, f32[8,3,128,128]{3,2,0,1:T(8,128)S(1)}, s32[8,128,128]{2,1,0:T(8,128)}, f32[8,3,128,128]{3,2,0,1:T(8,128)}, s32[]{:T(128)}) %tuple.61), condition=%wide.region_10.11_spmd, body=%wide.region_8.10_spmd.sunk | while | flops 14630914 | bytes 5570633 | solution.py:105
  290.7 2.8 iota_compare_fusion.8
  294.4 7.8 %select_reduce_fusion.5 = f32[3,128,128]{2,1,0:T(8,128)S(1)} fusion(f32[3,128,128]{2,1,0:T(8,128)S(1)} %dynamic-slice_bitcast_fusion.10, pred[128,128,128]{2,1,0:T(8,128)(4,1)S(1)} %iota_compare_fusion.8), kind=kLoop, calls=%fused_computation.12.clone.1 | loop fusion | flops 12533760 | bytes 2490368 | tf_op jit(solution)/shard_map/while/body/eval_jaxpr/reduce_sum | solution.py:103
  303.1 2.8 iota_compare_fusion.8
  306.9 7.8 %select_reduce_fusion.5 = f32[3,128,128]{2,1,0:T(8,128)S(1)} fusion(f32[3,128,128]{2,1,0:T(8,128)S(1)} %dynamic-slice_bitcast_fusion.10, pred[128,128,128]{2,1,0:T(8,128)(4,1)S(1)} %iota_compare_fusion.8), kind=kLoop, calls=%fused_computation.12.clone.1 | loop fusion | flops 12533760 | bytes 2490368 | tf_op jit(solution)/shard_map/while/body/eval_jaxpr/reduce_sum | solution.py:103
  315.6 2.8 iota_compare_fusion.8
  319.3 7.8 %select_reduce_fusion.5 = f32[3,128,128]{2,1,0:T(8,128)S(1)} fusion(f32[3,128,128]{2,1,0:T(8,128)S(1)} %dynamic-slice_bitcast_fusion.10, pred[128,128,128]{2,1,0:T(8,128)(4,1)S(1)} %iota_compare_fusion.8), kind=kLoop, calls=%fused_computation.12.clone.1 | loop fusion | flops 12533760 | bytes 2490368 | tf_op jit(solution)/shard_map/while/body/eval_jaxpr/reduce_sum | solution.py:103
  328.0 2.8 iota_compare_fusion.8
  331.7 7.8 %select_reduce_fusion.5 = f32[3,128,128]{2,1,0:T(8,128)S(1)} fusion(f32[3,128,128]{2,1,0:T(8,128)S(1)} %dynamic-slice_bitcast_fusion.10, pred[128,128,128]{2,1,0:T(8,128)(4,1)S(1)} %iota_compare_fusion.8), kind=kLoop, calls=%fused_computation.12.clone.1 | loop fusion | flops 12533760 | bytes 2490368 | tf_op jit(solution)/shard_map/while/body/eval_jaxpr/reduce_sum | solution.py:103
  340.4 2.8 iota_compare_fusion.8
  344.1 7.8 %select_reduce_fusion.5 = f32[3,128,128]{2,1,0:T(8,128)S(1)} fusion(f32[3,128,128]{2,1,0:T(8,128)S(1)} %dynamic-slice_bitcast_fusion.10, pred[128,128,128]{2,1,0:T(8,128)(4,1)S(1)} %iota_compare_fusion.8), kind=kLoop, calls=%fused_computation.12.clone.1 | loop fusion | flops 12533760 | bytes 2490368 | tf_op jit(solution)/shard_map/while/body/eval_jaxpr/reduce_sum | solution.py:103
  352.8 2.8 iota_compare_fusion.8
  356.6 7.8 %select_reduce_fusion.5 = f32[3,128,128]{2,1,0:T(8,128)S(1)} fusion(f32[3,128,128]{2,1,0:T(8,128)S(1)} %dynamic-slice_bitcast_fusion.10, pred[128,128,128]{2,1,0:T(8,128)(4,1)S(1)} %iota_compare_fusion.8), kind=kLoop, calls=%fused_computation.12.clone.1 | loop fusion | flops 12533760 | bytes 2490368 | tf_op jit(solution)/shard_map/while/body/eval_jaxpr/reduce_sum | solution.py:103
  365.2 2.8 iota_compare_fusion.8
  369.0 7.8 %select_reduce_fusion.5 = f32[3,128,128]{2,1,0:T(8,128)S(1)} fusion(f32[3,128,128]{2,1,0:T(8,128)S(1)} %dynamic-slice_bitcast_fusion.10, pred[128,128,128]{2,1,0:T(8,128)(4,1)S(1)} %iota_compare_fusion.8), kind=kLoop, calls=%fused_computation.12.clone.1 | loop fusion | flops 12533760 | bytes 2490368 | tf_op jit(solution)/shard_map/while/body/eval_jaxpr/reduce_sum | solution.py:103
  377.7 2.8 iota_compare_fusion.8
  381.4 7.8 %select_reduce_fusion.5 = f32[3,128,128]{2,1,0:T(8,128)S(1)} fusion(f32[3,128,128]{2,1,0:T(8,128)S(1)} %dynamic-slice_bitcast_fusion.10, pred[128,128,128]{2,1,0:T(8,128)(4,1)S(1)} %iota_compare_fusion.8), kind=kLoop, calls=%fused_computation.12.clone.1 | loop fusion | flops 12533760 | bytes 2490368 | tf_op jit(solution)/shard_map/while/body/eval_jaxpr/reduce_sum | solution.py:103
  389.2 1.8 fusion.12
  (104 shorter events, 40.8 us)
Async XLA Ops:
  0.6 20.3 %copy-start.1 = (f32[3,64,1024]{2,1,0:T(8,128)S(1)}, f32[3,64,1024]{2,1,0:T(8,128)}, u32[]{:S(2)}) copy-start(f32[3,64,1024]{2,1,0:T(8,128)} %param.13) | copy-start | bytes 2359300
  0.6 25.0 %copy-start.5 = (f32[2,64,1024]{2,1,0:T(8,128)S(1)}, f32[2,64,1024]{2,1,0:T(8,128)}, u32[]{:S(2)}) copy-start(f32[2,64,1024]{2,1,0:T(8,128)} %param.14) | copy-start | bytes 1572868
  1.7 19.2 %collective-permute-start = (f32[3,1,1024]{2,1,0:T(1,128)S(1)}, f32[3,1,1024]{2,1,0:T(1,128)S(1)}, u32[]{:S(2)}, u32[]{:S(2)}) collective-permute-start(f32[3,1,1024]{2,1,0:T(1,128)S(1)} %get-tuple-element.98), channel_id=1, source_target_pairs={{0,4},{4,8},{8,12},{12,16},{16,20},{20,24},{24,28},{1,5},{5,9},{9,... | collective-permute-start | bytes 36872 | tf_op jit(solution)/shard_map/ppermute | solution.py:21
  6.2 14.6 %collective-permute-start.1 = (f32[3,1,1024]{2,1,0:T(1,128)S(1)}, f32[3,1,1024]{2,1,0:T(1,128)S(1)}, u32[]{:S(2)}, u32[]{:S(2)}) collective-permute-start(f32[3,1,1024]{2,1,0:T(1,128)S(1)} %get-tuple-element.99), channel_id=1, source_target_pairs={{4,0},{8,4},{12,8},{16,12},{20,16},{24,20},{28,24},{5,1},{9,5},{13... | collective-permute-start | bytes 36872 | tf_op jit(solution)/shard_map/ppermute | solution.py:24
  14.6 42.3 %all-to-all-start = ((s32[32,32,128]{2,1,0:T(8,128)}), s32[32,32,128]{2,1,0:T(8,128)S(1)}, u32[]{:S(2)}, u32[]{:S(2)}) async-start(s32[32,32,128]{2,1,0:T(8,128)} %bitcast.13), calls=%async_computation | async-start | bytes 1048576 | tf_op jit(solution)/shard_map/all_to_all | solution.py:137
  21.0 10.9 %collective-permute-start.2 = (f32[3,66,1]{2,1,0:T(8,128)S(1)}, f32[3,66,1]{2,1,0:T(8,128)S(1)}, u32[]{:S(2)}, u32[]{:S(2)}) collective-permute-start(f32[3,66,1]{2,1,0:T(8,128)S(1)} %get-tuple-element.92), channel_id=1, source_target_pairs={{0,1},{1,2},{2,3},{4,5},{5,6},{6,7},{8,9},{9,10},{10,11},{12,13},{... | collective-permute-start | bytes 2384 | tf_op jit(solution)/shard_map/ppermute | solution.py:21
  24.3 7.6 %collective-permute-start.3 = (f32[3,66,1]{2,1,0:T(8,128)S(1)}, f32[3,66,1]{2,1,0:T(8,128)S(1)}, u32[]{:S(2)}, u32[]{:S(2)}) collective-permute-start(f32[3,66,1]{2,1,0:T(8,128)S(1)} %get-tuple-element.93), channel_id=1, source_target_pairs={{1,0},{2,1},{3,2},{5,4},{6,5},{7,6},{9,8},{10,9},{11,10},{13,12},{... | collective-permute-start | bytes 2384 | tf_op jit(solution)/shard_map/ppermute | solution.py:24
  32.7 6.9 %collective-permute-start.4 = (f32[3,1,1024]{2,1,0:T(1,128)S(1)}, f32[3,1,1024]{2,1,0:T(1,128)S(1)}, u32[]{:S(2)}, u32[]{:S(2)}) collective-permute-start(f32[3,1,1024]{2,1,0:T(1,128)S(1)} %get-tuple-element.96), channel_id=1, source_target_pairs={{0,4},{4,8},{8,12},{12,16},{16,20},{20,24},{24,28},{1,5},{5,9},{9,... | collective-permute-start | bytes 36872 | tf_op jit(solution)/shard_map/ppermute | solution.py:21
  37.6 5.0 %collective-permute-start.5 = (f32[3,1,1024]{2,1,0:T(1,128)S(1)}, f32[3,1,1024]{2,1,0:T(1,128)S(1)}, u32[]{:S(2)}, u32[]{:S(2)}) collective-permute-start(f32[3,1,1024]{2,1,0:T(1,128)S(1)} %get-tuple-element.97), channel_id=1, source_target_pairs={{4,0},{8,4},{12,8},{16,12},{20,16},{24,20},{28,24},{5,1},{9,5},{13... | collective-permute-start | bytes 36872 | tf_op jit(solution)/shard_map/ppermute | solution.py:24
  42.8 8.5 %collective-permute-start.6 = (f32[3,66,1]{2,1,0:T(8,128)S(1)}, f32[3,66,1]{2,1,0:T(8,128)S(1)}, u32[]{:S(2)}, u32[]{:S(2)}) collective-permute-start(f32[3,66,1]{2,1,0:T(8,128)S(1)} %get-tuple-element.90), channel_id=1, source_target_pairs={{0,1},{1,2},{2,3},{4,5},{5,6},{6,7},{8,9},{9,10},{10,11},{12,13},{... | collective-permute-start | bytes 2384 | tf_op jit(solution)/shard_map/ppermute | solution.py:21
  49.5 5.6 %collective-permute-start.7 = (f32[3,66,1]{2,1,0:T(8,128)S(1)}, f32[3,66,1]{2,1,0:T(8,128)}, u32[]{:S(2)}, u32[]{:S(2)}) collective-permute-start(f32[3,66,1]{2,1,0:T(8,128)S(1)} %get-tuple-element.91), channel_id=1, source_target_pairs={{1,0},{2,1},{3,2},{5,4},{6,5},{7,6},{9,8},{10,9},{11,10},{13,12},{... | collective-permute-start | bytes 2384 | tf_op jit(solution)/shard_map/ppermute | solution.py:24
  148.7 1.3 copy-start.3
  150.0 3.5 copy-start
  150.0 5.1 %copy-start.6 = (s32[128,2]{0,1:T(2,128)S(1)}, s32[128,2]{0,1:T(2,128)}, u32[]{:S(2)}) copy-start(s32[128,2]{0,1:T(2,128)} %param.19) | copy-start | bytes 3076
  150.0 47.2 %all-to-all-start.1 = ((f32[3,32,32,128]{3,2,0,1:T(8,128)}), f32[3,32,32,128]{3,2,0,1:T(8,128)}, u32[]{:S(2)}, u32[]{:S(2)}) async-start(f32[3,32,32,128]{3,2,0,1:T(8,128)} %copy.70), calls=%async_computation.1 | async-start | bytes 3145728 | tf_op jit(solution)/shard_map/all_to_all | solution.py:149
  197.2 8.1 %copy-start.4 = (f32[512,2,128]{2,1,0:T(2,128)S(1)}, f32[512,2,128]{2,1,0:T(2,128)}, u32[]{:S(2)}) copy-start(f32[512,2,128]{2,1,0:T(2,128)} %param.16) | copy-start | bytes 1572868
  245.2 5.9 %copy-start.2 = (f32[512,3,128]{2,1,0:T(4,128)S(1)}, f32[512,3,128]{2,1,0:T(4,128)}, u32[]{:S(2)}) copy-start(f32[512,3,128]{2,1,0:T(4,128)} %get-tuple-element.94) | copy-start | bytes 2359300
  245.2 43.2 %all-to-all-start.2 = ((f32[3,32,32,128]{3,2,0,1:T(8,128)}), f32[3,32,32,128]{3,2,0,1:T(8,128)S(1)}, u32[]{:S(2)}, u32[]{:S(2)}) async-start(f32[3,32,32,128]{3,2,0,1:T(8,128)} %copy.73), calls=%async_computation.2 | async-start | bytes 3145728 | tf_op jit(solution)/shard_map/all_to_all | solution.py:156
where the time goes:
time: 396 us; the launch traced here: 392 us
  other arithmetic  192 us (48%)
  local copies, waits for them, and re-layouts  77.5 us (20%)
  waiting for transfers between devices  50.1 us (13%)
  starting transfers between devices  41.5 us (10%)
  matrix products  29.3 us (7%)
    reduce_sum x8, other arithmetic, spread(): jnp.sum(jnp.where(matches[None], item[0][:, :, :, None], 0.0), axis=2)  62.4 us
    reduce_sum x8, other arithmetic, pick(): jnp.sum(jnp.where(matches[None], item[0][:, :, None, :], 0.0), axis=3)  55.6 us
    all_to_all x1, waiting for transfers between devices, on_device(): lax.all_to_all(outgoing, ('slab', 'pblk'), split_axis=1, concat_axis=1, t...  36.4 us
    scatter x1, local copies, waits for them, and re-layouts, on_device(): jnp.zeros((3, slot_total, BLOCK), jnp.float32).at[:, slot_of]  31.4 us
    eq x8, other arithmetic, pick(): item[1][:, :, None]  22.2 us
    eq x8, other arithmetic, spread(): item[1][:, :, None]  22.1 us
    ppermute x4, starting transfers between devices, padded_2(): lax.ppermute(lax.slice_in_dim(block, block.shape[dim] - width, None, axis...  19.5 us
    dot_general x1, matrix products, contact_terms(): jnp.einsum('pij,pcj->pci', weight, second_block, precision=lax.Precision....  15.4 us
  transfers between devices with their start and end apart: 11, of which 5 were waited for; matrix products, arithmetic and copies ran while one was open for 14% of the time, Pallas kernels for 0%

commit v1 on v0

v1 whole, which is shorter than its diff:
```python
import jax
import jax.numpy as jnp
from jax import lax
from jax.experimental import pallas as pl
from jax.experimental.pallas import tpu as pltpu
from jax.sharding import PartitionSpec as P

TIME_STEP = 0.2
VISCOSITY = 0.25
LOADING = 0.5
DAMPING = 0.1
LANES = 128
VMEM_BYTES = 48 * 1024 * 1024
BF = jnp.bfloat16
F32 = jnp.float32
NT = (((1,), (1,)), ((), ()))
NN = (((1,), (0,)), ((), ()))


def dot(a, b, dims=NN):
    return lax.dot_general(a, b, dims, preferred_element_type=F32)


def split(x):
    high = x.astype(BF)
    return high, (x - high.astype(F32)).astype(BF)


def select_rows(one_hot, values):
    high, low = split(values)
    return dot(one_hot, high) + dot(one_hot, low)


def tendency(v, xlo, xhi, wlo, whi, drift_x, drift_w):
    rows, cols = v.shape
    row = lax.broadcasted_iota(jnp.int32, v.shape, 0)
    col = lax.broadcasted_iota(jnp.int32, v.shape, 1)
    west = jnp.where(row == 0, xlo, pltpu.roll(v, 1, 0))
    east = jnp.where(row == rows - 1, xhi, pltpu.roll(v, rows - 1, 0))
    south = jnp.where(col == 0, wlo, pltpu.roll(v, 1, 1))
    north = jnp.where(col == cols - 1, whi, pltpu.roll(v, cols - 1, 1))
    upwind = drift_x * (v - west) + drift_w * (v - south)
    return VISCOSITY * (west + east + south + north - 4.0 * v) - upwind


def halo_terms(k, v, xlo, xhi, wlo, whi, drift):
    return tendency(
        v, xlo[k], xhi[k], wlo[k, :, LANES - 1 : LANES], whi[k, :, 0:1], drift[0], drift[1]
    )


def first_kernel(gas, drift, xlo, xhi, wlo, whi, out):
    for k in range(3):
        v = gas[k]
        out[k] = v + TIME_STEP * halo_terms(k, v, xlo, xhi, wlo, whi, drift)


def second_kernel(gas, one, drift, xlo, xhi, wlo, whi, tiles, out, sent, table):
    _, rows, cols = gas.shape
    per_row = cols // LANES
    for k in range(3):
        v = one[k]
        two = 0.5 * (gas[k] + v + TIME_STEP * halo_terms(k, v, xlo, xhi, wlo, whi, drift))
        out[k] = two
        for j in range(per_row):
            table[k, pl.ds(j, rows, stride=per_row), :] = two[:, j * LANES : (j + 1) * LANES]
    count = table.shape[1]
    slots = tiles.shape[0]
    one_hot = (
        tiles[...] == lax.broadcasted_iota(jnp.int32, (slots, count), 1)
    ).astype(F32).astype(BF)
    for k in range(3):
        sent[:, k * LANES : (k + 1) * LANES] = select_rows(one_hot, table[k])


def contact_kernel(pairs, particles, contact, acc, parts):
    step = pl.program_id(0)
    group = contact.shape[0]

    @pl.when(step == 0)
    def _():
        acc[...] = jnp.zeros_like(acc)
        parts[...] = jnp.ones_like(parts)
        for k in range(3):
            high, low = split(particles[:, k, :])
            parts[:, k, :] = high.astype(F32)
            parts[:, k + 3, :] = low.astype(F32)

    for r in range(group):
        at = (step * group + r) * 2
        a, b = pairs[at], pairs[at + 1]
        weight = contact[r].astype(F32).astype(BF)
        part_a, part_b = parts[a], parts[b]
        gain_a = dot(part_b.astype(BF), weight, NT)
        gain_b = dot(part_a.astype(BF), weight, NN)
        acc[a] = acc[a] + (gain_a - gain_a[6:7] * part_a)
        acc[b] = acc[b] + (gain_b - gain_b[6:7] * part_b)


def terms_kernel(got, slot_col, slot_row, cells, particles, rates, acc, sent, out, terms, spread):
    slots = got.shape[0]
    blocks = cells.shape[0]
    one_hot = (
        slot_col[...] == lax.broadcasted_iota(jnp.int32, (blocks, slots), 1)
    ).astype(F32).astype(BF)
    offsets = jnp.bitwise_and(cells[...], LANES - 1)
    for k in range(3):
        tile = select_rows(one_hot, got[:, k * LANES : (k + 1) * LANES])
        picked = jnp.take_along_axis(tile, offsets, axis=1)
        state = particles[:, k, :]
        term = rates[:, k // 2, :] * (picked - state)
        force = DAMPING * (acc[:, k, :] + acc[:, k + 3, :])
        out[:, k, :] = state + TIME_STEP * (term + force)
        high, low = split(term)
        terms[:, k, :] = high.astype(F32)
        terms[:, k + 3, :] = low.astype(F32)
    for k in (6, 7):
        terms[:, k, :] = jnp.zeros((blocks, LANES), F32)
    lane_of = lax.broadcasted_iota(jnp.int32, (LANES, LANES), 0)

    def one_group(step, carry):
        base = pl.multiple_of(step * 8, 8)
        near = jnp.bitwise_and(cells[pl.ds(base, 8), :], LANES - 1)
        for r in range(8):
            match = (near[r : r + 1] == lane_of).astype(F32).astype(BF)
            spread[base + r] = dot(terms[base + r].astype(BF), match, NT)
        return carry

    lax.fori_loop(0, blocks // 8, one_group, 0)
    into = (
        slot_row[...] == lax.broadcasted_iota(jnp.int32, (slots, blocks), 0)
    ).astype(F32).astype(BF)
    for k in range(3):
        summed = spread[:, k, :] + spread[:, k + 3, :]
        sent[:, k * LANES : (k + 1) * LANES] = select_rows(into, summed)


def sources_kernel(got, tiles, two, out, sums):
    _, rows, cols = two.shape
    per_row = cols // LANES
    slots = got.shape[0]
    count = sums.shape[1]
    one_hot = (
        tiles[...] == lax.broadcasted_iota(jnp.int32, (count, slots), 0)
    ).astype(F32).astype(BF)
    for k in range(3):
        sums[k] = select_rows(one_hot, got[:, k * LANES : (k + 1) * LANES])
        for j in range(per_row):
            cols_j = slice(j * LANES, (j + 1) * LANES)
            out[k, :, cols_j] = two[k, :, cols_j] - (TIME_STEP * LOADING) * sums[
                k, pl.ds(j, rows, stride=per_row), :
            ]


def params():
    return pltpu.CompilerParams(vmem_limit_bytes=VMEM_BYTES)


def cost(flops, moved):
    return pl.CostEstimate(flops=flops, bytes_accessed=moved, transcendentals=0)


def halos(v):
    found = []
    for axis, dim, width in (("slab", 1, 1), ("pblk", 2, LANES)):
        count = lax.axis_size(axis)
        up = [(i, i + 1) for i in range(count - 1)]
        down = [(i + 1, i) for i in range(count - 1)]
        size = v.shape[dim]
        found.append(lax.ppermute(lax.slice_in_dim(v, size - width, size, axis=dim), axis, up))
        found.append(lax.ppermute(lax.slice_in_dim(v, 0, width, axis=dim), axis, down))
    return found


def exchange(x):
    return lax.all_to_all(x, ("slab", "pblk"), split_axis=0, concat_axis=0, tiled=True)


def on_device(gas, drift, particles, rates, owner, cells, pairs, contact):
    devices = lax.axis_size("slab") * lax.axis_size("pblk")
    blocks = cells.shape[0]
    depth = max(2, 2 * blocks // devices)
    slots = devices * depth
    tile_count = gas.shape[1] * gas.shape[2] // LANES
    target = owner[:, 0]
    before = jnp.arange(blocks)[None, :] < jnp.arange(blocks)[:, None]
    same = target[None, :] == target[:, None]
    position = jnp.sum((before & same).astype(jnp.int32), axis=1)
    slot = target * depth + position
    tile = cells[:, 0] // LANES
    asked = jnp.sum(
        jnp.where(slot[None, :] == jnp.arange(slots)[:, None], tile[None, :], 0), axis=1
    ).reshape(devices, depth)
    tiles = exchange(asked).reshape(slots)

    field = jax.ShapeDtypeStruct(gas.shape, F32)
    wide = jax.ShapeDtypeStruct((slots, 3 * LANES), F32)
    one = pl.pallas_call(first_kernel, out_shape=field, compiler_params=params())(
        gas, drift, *halos(gas)
    )
    two, sent_gas = pl.pallas_call(
        second_kernel,
        out_shape=(field, wide),
        scratch_shapes=[pltpu.VMEM((3, tile_count, LANES), F32)],
        compiler_params=params(),
    )(gas, one, drift, *halos(one), tiles[:, None])
    got_gas = exchange(sent_gas)

    pair_count = contact.shape[0]
    group = 8
    acc = pl.pallas_call(
        contact_kernel,
        grid_spec=pltpu.PrefetchScalarGridSpec(
            num_scalar_prefetch=1,
            grid=(pair_count // group,),
            in_specs=[
                pl.BlockSpec(particles.shape, lambda i, s: (0, 0, 0)),
                pl.BlockSpec((group, LANES, LANES), lambda i, s: (i, 0, 0)),
            ],
            out_specs=pl.BlockSpec((blocks, 8, LANES), lambda i, s: (0, 0, 0)),
            scratch_shapes=[pltpu.VMEM((blocks, 8, LANES), F32)],
        ),
        out_shape=jax.ShapeDtypeStruct((blocks, 8, LANES), F32),
        compiler_params=params(),
        cost_estimate=cost(pair_count * 4 * 8 * LANES * LANES, 3 * contact.size * 4),
    )(pairs.reshape(-1), particles, contact)

    sent_terms, particles_next = pl.pallas_call(
        terms_kernel,
        out_shape=(wide, jax.ShapeDtypeStruct(particles.shape, F32)),
        scratch_shapes=[pltpu.VMEM((blocks, 8, LANES), F32)] * 2,
        compiler_params=params(),
    )(got_gas, slot[:, None], slot[None, :], cells, particles, rates, acc)
    gas_next = pl.pallas_call(
        sources_kernel,
        out_shape=field,
        scratch_shapes=[pltpu.VMEM((3, tile_count, LANES), F32)],
        compiler_params=params(),
    )(exchange(sent_terms), tiles[None, :], two)
    return gas_next, particles_next


def solution(mesh):
    own = ("slab", "pblk")
    grid = P(None, "slab", "pblk")
    in_specs = (
        grid,
        grid,
        P(own, None, None),
        P(own, None, None),
        P(own, None),
        P(own, None),
        P(own, None),
        P(own, None, None),
    )
    return jax.shard_map(
        on_device,
        mesh=mesh,
        in_specs=in_specs,
        out_specs=(grid, P(own, None, None)),
        check_vma=False,
    )
```

time: 396 us -> 165 us (0.42)
  other arithmetic: 192 us -> 2.84 us
  local copies, waits for them, and re-layouts: 77.5 us -> 15.2 us
  Pallas kernels: 0 us -> 46.6 us
  matrix products: 29.3 us -> 0 us
  blocking collectives: 0 us -> 12 us
  starting transfers between devices: 41.5 us -> 29.5 us
  waiting for transfers between devices: 50.1 us -> 57.3 us
    reduce_sum x18 -> x2, other arithmetic: 125 us -> 1.3 us  [the longest x1 1.01 us: on_device(): position = jnp.sum((before & same).astype(jnp.int32), axis=1)]
    pallas_call x0 -> x5, Pallas kernels: none -> 46.6 us  [the longest x1 27 us: on_device(): pl.pallas_call(terms_kernel, out_shape=(wide, jax.ShapeDtypeStruct(partic...]
    eq x16 -> x0, other arithmetic: 44.3 us -> none  [the longest x8 22.2 us: pick(): item[1][:, :, None]]
    scatter x2 -> x0, local copies, waits for them, and re-layouts: 34.2 us -> none  [the longest x1 31.4 us: on_device(): jnp.zeros((3, slot_total, BLOCK), jnp.float32).at[:, slot_of]]
    dot_general x4 -> x0, matrix products: 29.3 us -> none  [the longest x1 15.4 us: contact_terms(): jnp.einsum('pij,pcj->pci', weight, second_block, precision=lax.Precision....]
    all_to_all x3 -> x2, waiting for transfers between devices: 36.4 us -> 57.3 us  [exchange(): lax.all_to_all(x, ('slab', 'pblk'), split_axis=0, concat_axis=0, tiled=True)]
    broadcast_in_dim x18 -> x0, local copies, waits for them, and re-layouts: 15.6 us -> none  [the longest x8 7.61 us: spread(): jnp.where(matches[None], item[0][:, :, :, None], 0.0)]
    ppermute x8, waiting for transfers between devices: 13.7 us -> 0.02 us  [the longest x4 0.01 us: halos(): lax.ppermute(lax.slice_in_dim(v, 0, width, axis=dim), axis, down)]
  transfers between devices with their start and end apart: 11 -> 10, of which waited for: 5 -> 2; matrix products, arithmetic and copies ran while one was open for 14% -> 5% of each run, Pallas kernels for 0% -> 8%
where the time goes in v1:
time: 165 us; the launch traced here: 164 us
  waiting for transfers between devices  57.3 us (35%)
  Pallas kernels  46.6 us (28%)
  starting transfers between devices  29.5 us (18%)
  local copies, waits for them, and re-layouts  15.2 us (9%)
  blocking collectives  12 us (7%)
  other arithmetic  2.84 us (2%)
    all_to_all x2, waiting for transfers between devices, exchange(): lax.all_to_all(x, ('slab', 'pblk'), split_axis=0, concat_axis=0, tiled=True)  57.3 us
    pallas_call x1, Pallas kernels, on_device(): pl.pallas_call(terms_kernel, out_shape=(wide, jax.ShapeDtypeStruct(partic...  27 us
    ppermute x4, starting transfers between devices, halos(): lax.ppermute(lax.slice_in_dim(v, size - width, size, axis=dim), axis, up)  16.1 us
    pallas_call x1, Pallas kernels, on_device(): pl.pallas_call(contact_kernel, grid_spec=pltpu.PrefetchScalarGridSpec(num...  13.9 us
    all_to_all x1, blocking collectives, exchange(): lax.all_to_all(x, ('slab', 'pblk'), split_axis=0, concat_axis=0, tiled=True)  12 us
    unnamed x32, local copies, waits for them, and re-layouts  10.6 us
    all_to_all x2, starting transfers between devices, exchange(): lax.all_to_all(x, ('slab', 'pblk'), split_axis=0, concat_axis=0, tiled=True)  6.96 us
    ppermute x4, starting transfers between devices, halos(): lax.ppermute(lax.slice_in_dim(v, 0, width, axis=dim), axis, down)  6.47 us
  transfers between devices with their start and end apart: 10, of which 2 were waited for; matrix products, arithmetic and copies ran while one was open for 5% of the time, Pallas kernels for 8%

profile of v1, /device:TPU:1, one launch (start us, length us, event | category | flops | bytes accessed | tf_op | source)
XLA Modules:
  0.0 164.5 jit_solution(12956024178671960128)
XLA Ops:
  0.6 0.0 copy-start.4
  0.6 1.0 fusion.6
  1.7 2.0 %collective-permute-start.1 = (f32[3,1,1024]{2,1,0:T(1,128)S(1)}, f32[3,1,1024]{2,1,0:T(1,128)S(1)}, u32[]{:S(2)}, u32[]{:S(2)}) collective-permute-start(f32[3,1,1024]{2,1,0:T(1,128)S(1)} %get-tuple-element.26), channel_id=1, source_target_pairs={{4,0},{8,4},{12,8},{16,12},{20,16},{24,20},{28,24},{5,1},{9,5},{13... | collective-permute-start | bytes 36872 | tf_op jit(solution)/shard_map/ppermute | solution.py:171
  3.6 4.5 %collective-permute-start = (f32[3,1,1024]{2,1,0:T(1,128)S(1)}, f32[3,1,1024]{2,1,0:T(1,128)S(1)}, u32[]{:S(2)}, u32[]{:S(2)}) collective-permute-start(f32[3,1,1024]{2,1,0:T(1,128)S(1)} %get-tuple-element.27), channel_id=1, source_target_pairs={{0,4},{4,8},{8,12},{12,16},{16,20},{20,24},{24,28},{1,5},{5,9},{9,... | collective-permute-start | bytes 36872 | tf_op jit(solution)/shard_map/ppermute | solution.py:170
  8.1 1.0 fusion.5
  9.1 1.3 collective-permute-start.3
  10.4 4.0 %collective-permute-start.2 = (f32[3,64,128]{2,1,0:T(8,128)S(1)}, f32[3,64,128]{2,1,0:T(8,128)S(1)}, u32[]{:S(2)}, u32[]{:S(2)}) collective-permute-start(f32[3,64,128]{2,1,0:T(8,128)S(1)} %get-tuple-element.25), channel_id=1, source_target_pairs={{0,1},{1,2},{2,3},{4,5},{5,6},{6,7},{8,9},{9,10},{10,11},{12,13},{... | collective-permute-start | bytes 294920 | tf_op jit(solution)/shard_map/ppermute | solution.py:170
  14.4 1.0 convert_reduce_fusion
  15.4 1.1 slice_reduce_fusion
  16.5 0.7 add_select_fusion
  17.2 0.0 collective-permute-done.1.xhi
  17.2 0.0 collective-permute-done.xlo
  17.2 0.0 collective-permute-done.3.whi
  17.2 0.0 collective-permute-done.2.wlo
  17.2 0.0 copy-start.1
  17.2 1.1 copy-done.1
  18.3 1.0 copy-done.3
  19.4 0.6 shard_map.95.one
  20.1 1.9 %collective-permute-start.5 = (f32[3,1,1024]{2,1,0:T(1,128)S(1)}, f32[3,1,1024]{2,1,0:T(1,128)S(1)}, u32[]{:S(2)}, u32[]{:S(2)}) collective-permute-start(f32[3,1,1024]{2,1,0:T(1,128)S(1)} %get-tuple-element.22), channel_id=1, source_target_pairs={{4,0},{8,4},{12,8},{16,12},{20,16},{24,20},{28,24},{5,1},{9,5},{13... | collective-permute-start | bytes 36872 | tf_op jit(solution)/shard_map/ppermute | solution.py:171
  22.0 3.6 %collective-permute-start.4 = (f32[3,1,1024]{2,1,0:T(1,128)S(1)}, f32[3,1,1024]{2,1,0:T(1,128)S(1)}, u32[]{:S(2)}, u32[]{:S(2)}) collective-permute-start(f32[3,1,1024]{2,1,0:T(1,128)S(1)} %get-tuple-element.23), channel_id=1, source_target_pairs={{0,4},{4,8},{8,12},{12,16},{16,20},{20,24},{24,28},{1,5},{5,9},{9,... | collective-permute-start | bytes 36872 | tf_op jit(solution)/shard_map/ppermute | solution.py:170
  25.7 1.3 collective-permute-start.7
  27.0 4.0 %collective-permute-start.6 = (f32[3,64,128]{2,1,0:T(8,128)S(1)}, f32[3,64,128]{2,1,0:T(8,128)S(1)}, u32[]{:S(2)}, u32[]{:S(2)}) collective-permute-start(f32[3,64,128]{2,1,0:T(8,128)S(1)} %get-tuple-element.21), channel_id=1, source_target_pairs={{0,1},{1,2},{2,3},{4,5},{5,6},{6,7},{8,9},{9,10},{10,11},{12,13},{... | collective-permute-start | bytes 294920 | tf_op jit(solution)/shard_map/ppermute | solution.py:170
  31.0 0.3 select_reduce_fusion
  31.3 0.1 all_to_all.20
  31.4 12.0 %all_to_all.31 = s32[32,1,32]{2,1,0:T(1,128)S(1)} all-to-all(s32[32,1,32]{2,1,0:T(1,128)S(1)} %all_to_all.20), channel_id=1, replica_groups=mesh['slab'=8,'pblk'=4] {'slab','pblk'}, dimensions={0} | all-to-all | bytes 8192 | tf_op jit(solution)/shard_map/all_to_all | solution.py:176
  43.3 0.5 broadcast.52
  43.9 0.7 reduce.9
  44.6 0.5 broadcast_in_dim_reshape.8.tiles
  45.1 0.0 collective-permute-done.5.xhi
  45.1 0.0 collective-permute-done.4.xlo
  45.1 0.0 collective-permute-done.7.whi
  45.1 0.0 collective-permute-done.6.wlo
  45.1 0.0 copy-done.4
  45.1 0.0 copy-done.2
  45.2 2.3 %shard_map.96 = (f32[3,64,1024]{2,1,0:T(8,128)S(1)}, f32[1024,384]{1,0:T(8,128)S(1)}) custom-call(f32[3,64,1024]{2,1,0:T(8,128)S(1)} %copy-done.2, f32[3,64,1024]{2,1,0:T(8,128)S(1)} %shard_map.95.one, f32[2,64,1024]{2,1,0:T(8,128)S(1)} %copy-done.4, f32[3,1,1024]{2,1,0:T(1,128)S(1)} %collective-permute-done.4.xlo, ...), custom_call_target="tpu_custom_call" | custom-call | tf_op jit(solution)/shard_map/pallas_call | solution.py:201
  47.5 0.0 copy-start.5
  47.5 1.2 copy-done.5
  48.7 0.9 copy-done.8
  49.6 3.8 %all-to-all-start.1 = ((f32[32,32,384]{2,1,0:T(8,128)}), f32[32,32,384]{2,1,0:T(8,128)}, u32[]{:S(2)}, u32[]{:S(2)}) async-start(f32[32,32,384]{2,1,0:T(8,128)} %bitcast.10), calls=%async_computation.1 | async-start | bytes 3145728 | tf_op jit(solution)/shard_map/all_to_all | solution.py:176
  53.4 0.0 copy-done.12
  53.4 0.1 copy.36
  53.6 0.0 copy-done.13
  53.6 0.1 copy.39
  53.7 0.1 reshape.67.pairs
  53.8 0.1 copy.38
  54.0 0.0 copy-done.11
  54.0 0.5 copy.41.particles
  54.5 0.1 multiply_reduce_fusion
  54.7 0.0 copy-start.7
  54.7 13.9 %shard_map.97.acc = f32[512,8,128]{2,1,0:T(8,128)S(1)} custom-call(s32[256]{0:T(256)S(1)} %reshape.67.pairs, f32[512,3,128]{2,1,0:T(4,128)S(1)} %copy.41.particles, s32[128,128,128]{2,1,0:T(8,128)} %contact.1), custom_call_target="tpu_custom_call" | custom-call | flops 67108864 | bytes 25165824 | tf_op jit(solution)/shard_map/pallas_call | solution.py:211
  68.6 0.0 copy-start
  68.7 1.3 copy-done
  70.0 21.0 %all-to-all-done.1 = f32[32,32,384]{2,1,0:T(8,128)} async-done(((f32[32,32,384]{2,1,0:T(8,128)}), f32[32,32,384]{2,1,0:T(8,128)}, u32[]{:S(2)}, u32[]{:S(2)}) %all-to-all-start.1) | async-done | bytes 1572896 | tf_op jit(solution)/shard_map/all_to_all | solution.py:176
  90.9 0.0 copy-done.7
  91.0 1.0 copy-done.10
  92.0 27.0 %shard_map.98 = (f32[1024,384]{1,0:T(8,128)S(1)}, f32[512,3,128]{2,1,0:T(4,128)S(1)}) custom-call(f32[1024,384]{1,0:T(8,128)} %bitcast.2.got, s32[512,1]{1,0:T(8,128)S(1)} %get-tuple-element.29.slot_col, s32[1,512]{1,0:T(1,128)S(1)} %add.23.slot_row, s32[512,128]{1,0:T(8,128)S(1)} %copy-done.7, f32[512,3,128]{2,1,0:T(4,128)S(1)} %copy.41.particles, ...), custom_call_target="tpu_custom_call" | custom-call | tf_op jit(solution)/shard_map/pallas_call | solution.py:228
  119.0 0.0 copy-start.6
  119.0 1.2 copy-done.6
  120.2 3.1 %all-to-all-start.2 = ((f32[32,32,384]{2,1,0:T(8,128)}), f32[32,32,384]{2,1,0:T(8,128)S(1)}, u32[]{:S(2)}, u32[]{:S(2)}) async-start(f32[32,32,384]{2,1,0:T(8,128)} %bitcast.11), calls=%async_computation.2 | async-start | bytes 3145728 | tf_op jit(solution)/shard_map/all_to_all | solution.py:176
  123.3 0.1 broadcast_in_dim_reshape.7.tiles
  123.4 0.9 copy.42
  124.3 36.3 %all-to-all-done.2 = f32[32,32,384]{2,1,0:T(8,128)S(1)} async-done(((f32[32,32,384]{2,1,0:T(8,128)}), f32[32,32,384]{2,1,0:T(8,128)S(1)}, u32[]{:S(2)}, u32[]{:S(2)}) %all-to-all-start.2) | async-done | bytes 1572896 | tf_op jit(solution)/shard_map/all_to_all | solution.py:176
  160.6 1.1 copy-done.9
  161.8 2.7 %shard_map.99 = f32[3,64,1024]{2,1,0:T(8,128)} custom-call(f32[1024,384]{1,0:T(8,128)S(1)} %bitcast.9, s32[1,1024]{1,0:T(1,128)S(1)} %broadcast_in_dim_reshape.7.tiles, f32[3,64,1024]{2,1,0:T(8,128)S(1)} %copy-done.9), custom_call_target="tpu_custom_call" | custom-call | tf_op jit(solution)/shard_map/pallas_call | solution.py:234
  (11 shorter events, 0.1 us)
Async XLA Ops:
  0.6 44.5 %copy-start.4 = (f32[2,64,1024]{2,1,0:T(8,128)S(1)}, f32[2,64,1024]{2,1,0:T(8,128)}, u32[]{:S(2)}) copy-start(f32[2,64,1024]{2,1,0:T(8,128)} %drift.3) | copy-start | bytes 1572868
  1.7 15.5 %collective-permute-start.1 = (f32[3,1,1024]{2,1,0:T(1,128)S(1)}, f32[3,1,1024]{2,1,0:T(1,128)S(1)}, u32[]{:S(2)}, u32[]{:S(2)}) collective-permute-start(f32[3,1,1024]{2,1,0:T(1,128)S(1)} %get-tuple-element.26), channel_id=1, source_target_pairs={{4,0},{8,4},{12,8},{16,12},{20,16},{24,20},{28,24},{5,1},{9,5},{13... | collective-permute-start | bytes 36872 | tf_op jit(solution)/shard_map/ppermute | solution.py:171
  3.6 13.5 %collective-permute-start = (f32[3,1,1024]{2,1,0:T(1,128)S(1)}, f32[3,1,1024]{2,1,0:T(1,128)S(1)}, u32[]{:S(2)}, u32[]{:S(2)}) collective-permute-start(f32[3,1,1024]{2,1,0:T(1,128)S(1)} %get-tuple-element.27), channel_id=1, source_target_pairs={{0,4},{4,8},{8,12},{12,16},{16,20},{20,24},{24,28},{1,5},{5,9},{9,... | collective-permute-start | bytes 36872 | tf_op jit(solution)/shard_map/ppermute | solution.py:170
  9.1 8.1 %collective-permute-start.3 = (f32[3,64,128]{2,1,0:T(8,128)S(1)}, f32[3,64,128]{2,1,0:T(8,128)S(1)}, u32[]{:S(2)}, u32[]{:S(2)}) collective-permute-start(f32[3,64,128]{2,1,0:T(8,128)S(1)} %get-tuple-element.24), channel_id=1, source_target_pairs={{1,0},{2,1},{3,2},{5,4},{6,5},{7,6},{9,8},{10,9},{11,10},{13,12},{... | collective-permute-start | bytes 294920 | tf_op jit(solution)/shard_map/ppermute | solution.py:171
  10.4 6.8 %collective-permute-start.2 = (f32[3,64,128]{2,1,0:T(8,128)S(1)}, f32[3,64,128]{2,1,0:T(8,128)S(1)}, u32[]{:S(2)}, u32[]{:S(2)}) collective-permute-start(f32[3,64,128]{2,1,0:T(8,128)S(1)} %get-tuple-element.25), channel_id=1, source_target_pairs={{0,1},{1,2},{2,3},{4,5},{5,6},{6,7},{8,9},{9,10},{10,11},{12,13},{... | collective-permute-start | bytes 294920 | tf_op jit(solution)/shard_map/ppermute | solution.py:170
  17.2 1.1 copy-start.1
  18.3 1.0 copy-start.3
  19.4 25.8 %copy-start.2 = (f32[3,64,1024]{2,1,0:T(8,128)S(1)}, f32[3,64,1024]{2,1,0:T(8,128)}, u32[]{:S(2)}) copy-start(f32[3,64,1024]{2,1,0:T(8,128)} %gas.3) | copy-start | bytes 2359300
  20.1 25.0 %collective-permute-start.5 = (f32[3,1,1024]{2,1,0:T(1,128)S(1)}, f32[3,1,1024]{2,1,0:T(1,128)S(1)}, u32[]{:S(2)}, u32[]{:S(2)}) collective-permute-start(f32[3,1,1024]{2,1,0:T(1,128)S(1)} %get-tuple-element.22), channel_id=1, source_target_pairs={{4,0},{8,4},{12,8},{16,12},{20,16},{24,20},{28,24},{5,1},{9,5},{13... | collective-permute-start | bytes 36872 | tf_op jit(solution)/shard_map/ppermute | solution.py:171
  22.0 23.1 %collective-permute-start.4 = (f32[3,1,1024]{2,1,0:T(1,128)S(1)}, f32[3,1,1024]{2,1,0:T(1,128)S(1)}, u32[]{:S(2)}, u32[]{:S(2)}) collective-permute-start(f32[3,1,1024]{2,1,0:T(1,128)S(1)} %get-tuple-element.23), channel_id=1, source_target_pairs={{0,4},{4,8},{8,12},{12,16},{16,20},{20,24},{24,28},{1,5},{5,9},{9,... | collective-permute-start | bytes 36872 | tf_op jit(solution)/shard_map/ppermute | solution.py:170
  25.7 19.4 %collective-permute-start.7 = (f32[3,64,128]{2,1,0:T(8,128)S(1)}, f32[3,64,128]{2,1,0:T(8,128)S(1)}, u32[]{:S(2)}, u32[]{:S(2)}) collective-permute-start(f32[3,64,128]{2,1,0:T(8,128)S(1)} %get-tuple-element.20), channel_id=1, source_target_pairs={{1,0},{2,1},{3,2},{5,4},{6,5},{7,6},{9,8},{10,9},{11,10},{13,12},{... | collective-permute-start | bytes 294920 | tf_op jit(solution)/shard_map/ppermute | solution.py:171
  27.0 18.2 %collective-permute-start.6 = (f32[3,64,128]{2,1,0:T(8,128)S(1)}, f32[3,64,128]{2,1,0:T(8,128)S(1)}, u32[]{:S(2)}, u32[]{:S(2)}) collective-permute-start(f32[3,64,128]{2,1,0:T(8,128)S(1)} %get-tuple-element.21), channel_id=1, source_target_pairs={{0,1},{1,2},{2,3},{4,5},{5,6},{6,7},{8,9},{9,10},{10,11},{12,13},{... | collective-permute-start | bytes 294920 | tf_op jit(solution)/shard_map/ppermute | solution.py:170
  47.5 1.2 copy-start.5
  48.7 0.9 copy-start.8
  49.5 3.9 %copy-start.12 = (s32[512,1]{0,1:T(1,128)S(1)}, s32[512,1]{0,1:T(1,128)}, u32[]{:S(2)}) copy-start(s32[512,1]{0,1:T(1,128)} %param.12) | copy-start | bytes 6148
  49.6 4.0 %copy-start.13 = (s32[128,2]{0,1:T(2,128)S(1)}, s32[128,2]{0,1:T(2,128)}, u32[]{:S(2)}) copy-start(s32[128,2]{0,1:T(2,128)} %param.14) | copy-start | bytes 3076
  49.6 4.4 %copy-start.11 = (f32[512,3,128]{2,0,1:T(8,128)S(1)}, f32[512,3,128]{2,0,1:T(8,128)}, u32[]{:S(2)}) copy-start(f32[512,3,128]{2,0,1:T(8,128)} %param.10) | copy-start | bytes 2359300
  49.6 41.4 %all-to-all-start.1 = ((f32[32,32,384]{2,1,0:T(8,128)}), f32[32,32,384]{2,1,0:T(8,128)}, u32[]{:S(2)}, u32[]{:S(2)}) async-start(f32[32,32,384]{2,1,0:T(8,128)} %bitcast.10), calls=%async_computation.1 | async-start | bytes 3145728 | tf_op jit(solution)/shard_map/all_to_all | solution.py:176
  54.7 36.2 %copy-start.7 = (s32[512,128]{1,0:T(8,128)S(1)}, s32[512,128]{1,0:T(8,128)}, u32[]{:S(2)}) copy-start(s32[512,128]{1,0:T(8,128)} %cells.1) | copy-start | bytes 786436
  68.6 1.3 copy-start
  90.9 1.0 copy-start.10
  119.0 1.2 copy-start.6
  120.2 40.5 %all-to-all-start.2 = ((f32[32,32,384]{2,1,0:T(8,128)}), f32[32,32,384]{2,1,0:T(8,128)S(1)}, u32[]{:S(2)}, u32[]{:S(2)}) async-start(f32[32,32,384]{2,1,0:T(8,128)} %bitcast.11), calls=%async_computation.2 | async-start | bytes 3145728 | tf_op jit(solution)/shard_map/all_to_all | solution.py:176
  160.6 1.1 copy-start.9

commit v2 on v1

--- a/solution.py
+++ b/solution.py
@@ -97,7 +97,42 @@
         acc[b] = acc[b] + (gain_b - gain_b[6:7] * part_b)
 
 
-def terms_kernel(got, slot_col, slot_row, cells, particles, rates, acc, sent, out, terms, spread):
+def sums_kernel(slot_row, cells, particles, rates, rate_sums, state_sums, parts, spread):
+    slots = rate_sums.shape[0]
+    blocks = cells.shape[0]
+    parts[...] = jnp.zeros_like(parts)
+    for k in range(5):
+        value = rates[:, k, :] if k < 2 else rates[:, (k - 2) // 2, :] * particles[:, k - 2, :]
+        high, low = split(value)
+        parts[:, k, :] = high.astype(F32)
+        parts[:, k + 8, :] = low.astype(F32)
+    lane_of = lax.broadcasted_iota(jnp.int32, (LANES, LANES), 0)
+
+    def one_group(step, carry):
+        base = pl.multiple_of(step * 8, 8)
+        near = jnp.bitwise_and(cells[pl.ds(base, 8), :], LANES - 1)
+        for r in range(8):
+            match = (near[r : r + 1] == lane_of).astype(F32).astype(BF)
+            summed = dot(parts[base + r].astype(BF), match, NT)
+            spread[base + r] = summed[0:8] + summed[8:16]
+        return carry
+
+    lax.fori_loop(0, blocks // 8, one_group, 0)
+    into = (
+        slot_row[...] == lax.broadcasted_iota(jnp.int32, (slots, blocks), 0)
+    ).astype(F32).astype(BF)
+    for k in range(5):
+        moved = select_rows(into, spread[:, k, :])
+        if k == 0:
+            rate_sums[:, 0:LANES] = moved
+            rate_sums[:, LANES : 2 * LANES] = moved
+        elif k == 1:
+            rate_sums[:, 2 * LANES : 3 * LANES] = moved
+        else:
+            state_sums[:, (k - 2) * LANES : (k - 1) * LANES] = moved
+
+
+def particles_kernel(got, slot_col, cells, particles, rates, acc, out):
     slots = got.shape[0]
     blocks = cells.shape[0]
     one_hot = (
@@ -111,28 +146,6 @@
         term = rates[:, k // 2, :] * (picked - state)
         force = DAMPING * (acc[:, k, :] + acc[:, k + 3, :])
         out[:, k, :] = state + TIME_STEP * (term + force)
-        high, low = split(term)
-        terms[:, k, :] = high.astype(F32)
-        terms[:, k + 3, :] = low.astype(F32)
-    for k in (6, 7):
-        terms[:, k, :] = jnp.zeros((blocks, LANES), F32)
-    lane_of = lax.broadcasted_iota(jnp.int32, (LANES, LANES), 0)
-
-    def one_group(step, carry):
-        base = pl.multiple_of(step * 8, 8)
-        near = jnp.bitwise_and(cells[pl.ds(base, 8), :], LANES - 1)
-        for r in range(8):
-            match = (near[r : r + 1] == lane_of).astype(F32).astype(BF)
-            spread[base + r] = dot(terms[base + r].astype(BF), match, NT)
-        return carry
-
-    lax.fori_loop(0, blocks // 8, one_group, 0)
-    into = (
-        slot_row[...] == lax.broadcasted_iota(jnp.int32, (slots, blocks), 0)
-    ).astype(F32).astype(BF)
-    for k in range(3):
-        summed = spread[:, k, :] + spread[:, k + 3, :]
-        sent[:, k * LANES : (k + 1) * LANES] = select_rows(into, summed)
 
 
 def sources_kernel(got, tiles, two, out, sums):
@@ -204,7 +217,18 @@
         scratch_shapes=[pltpu.VMEM((3, tile_count, LANES), F32)],
         compiler_params=params(),
     )(gas, one, drift, *halos(one), tiles[:, None])
+    slot_row, sent_gas = lax.optimization_barrier((slot[None, :], sent_gas))
+    rate_sums, state_sums = pl.pallas_call(
+        sums_kernel,
+        out_shape=(wide, wide),
+        scratch_shapes=[pltpu.VMEM((blocks, 16, LANES), F32), pltpu.VMEM((blocks, 8, LANES), F32)],
+        compiler_params=params(),
+        cost_estimate=cost(blocks * 32 * LANES * LANES, 80_000_000),
+    )(slot_row, cells, particles, rates)
     got_gas = exchange(sent_gas)
+    sent_terms = got_gas * rate_sums - state_sums
+    pairs, sent_terms = lax.optimization_barrier((pairs, sent_terms))
+    got_terms = exchange(sent_terms)
 
     pair_count = contact.shape[0]
     group = 8
@@ -225,18 +249,18 @@
         cost_estimate=cost(pair_count * 4 * 8 * LANES * LANES, 3 * contact.size * 4),
     )(pairs.reshape(-1), particles, contact)
 
-    sent_terms, particles_next = pl.pallas_call(
-        terms_kernel,
-        out_shape=(wide, jax.ShapeDtypeStruct(particles.shape, F32)),
-        scratch_shapes=[pltpu.VMEM((blocks, 8, LANES), F32)] * 2,
-        compiler_params=params(),
-    )(got_gas, slot[:, None], slot[None, :], cells, particles, rates, acc)
+    particles_next = pl.pallas_call(
+        particles_kernel,
+        out_shape=jax.ShapeDtypeStruct(particles.shape, F32),
+        compiler_params=params(),
+        cost_estimate=cost(blocks * slots * 12 * LANES, 10_000_000),
+    )(got_gas, slot[:, None], cells, particles, rates, acc)
     gas_next = pl.pallas_call(
         sources_kernel,
         out_shape=field,
         scratch_shapes=[pltpu.VMEM((3, tile_count, LANES), F32)],
         compiler_params=params(),
-    )(exchange(sent_terms), tiles[None, :], two)
+    )(got_terms, tiles[None, :], two)
     return gas_next, particles_next
 
 

time: 165 us -> 135 us (0.82)
  waiting for transfers between devices: 57.3 us -> 24.1 us
  blocking collectives: 12 us -> 0 us
  starting transfers between devices: 29.5 us -> 36.7 us
  Pallas kernels: 46.6 us -> 50.8 us
  other arithmetic: 2.84 us -> 6.66 us
    all_to_all x2 -> x3, waiting for transfers between devices: 57.3 us -> 24.1 us  [exchange(): lax.all_to_all(x, ('slab', 'pblk'), split_axis=0, concat_axis=0, tiled=True)]
    all_to_all x1 -> x0, blocking collectives: 12 us -> none  [exchange(): lax.all_to_all(x, ('slab', 'pblk'), split_axis=0, concat_axis=0, tiled=True)]
    all_to_all x2 -> x3, starting transfers between devices: 6.96 us -> 14.1 us  [exchange(): lax.all_to_all(x, ('slab', 'pblk'), split_axis=0, concat_axis=0, tiled=True)]
    sub x0 -> x1, other arithmetic: none -> 3.23 us  [on_device(): sent_terms = got_gas * rate_sums - state_sums]
    pallas_call x1 -> x2, Pallas kernels: 27 us -> 29.7 us  [the longest x1 24.1 us: on_device(): pl.pallas_call(sums_kernel, out_shape=(wide, wide), scratch_shapes=[pltpu...]
    unnamed x32 -> x27, local copies, waits for them, and re-layouts: 10.6 us -> 9.21 us
  transfers between devices with their start and end apart: 10 -> 11, of which waited for: 2 -> 2; matrix products, arithmetic and copies ran while one was open for 5% -> 8% of each run, Pallas kernels for 8% -> 33%
where the time goes in v2:
time: 135 us; the launch traced here: 134 us
  Pallas kernels  50.8 us (38%)
  starting transfers between devices  36.7 us (27%)
  waiting for transfers between devices  24.1 us (18%)
  local copies, waits for them, and re-layouts  14.6 us (11%)
  other arithmetic  6.66 us (5%)
    pallas_call x1, Pallas kernels, on_device(): pl.pallas_call(sums_kernel, out_shape=(wide, wide), scratch_shapes=[pltpu...  24.1 us
    all_to_all x3, waiting for transfers between devices, exchange(): lax.all_to_all(x, ('slab', 'pblk'), split_axis=0, concat_axis=0, tiled=True)  24.1 us
    ppermute x4, starting transfers between devices, halos(): lax.ppermute(lax.slice_in_dim(v, size - width, size, axis=dim), axis, up)  15.8 us
    all_to_all x3, starting transfers between devices, exchange(): lax.all_to_all(x, ('slab', 'pblk'), split_axis=0, concat_axis=0, tiled=True)  14.1 us
    pallas_call x1, Pallas kernels, on_device(): pl.pallas_call(contact_kernel, grid_spec=pltpu.PrefetchScalarGridSpec(num...  13.9 us
    unnamed x27, local copies, waits for them, and re-layouts  9.21 us
    ppermute x4, starting transfers between devices, halos(): lax.ppermute(lax.slice_in_dim(v, 0, width, axis=dim), axis, down)  6.72 us
    pallas_call x1, Pallas kernels, on_device(): pl.pallas_call(particles_kernel, out_shape=jax.ShapeDtypeStruct(particles...  5.53 us
  transfers between devices with their start and end apart: 11, of which 2 were waited for; matrix products, arithmetic and copies ran while one was open for 8% of the time, Pallas kernels for 33%

profile of v2, /device:TPU:1, one launch (start us, length us, event | category | flops | bytes accessed | tf_op | source)
XLA Modules:
  0.0 133.8 jit_solution(8496825500767691841)
XLA Ops:
  0.6 0.0 copy-start.1
  0.6 0.0 copy-start.3
  0.7 1.1 fusion.6
  1.7 2.0 %collective-permute-start.1 = (f32[3,1,1024]{2,1,0:T(1,128)S(1)}, f32[3,1,1024]{2,1,0:T(1,128)S(1)}, u32[]{:S(2)}, u32[]{:S(2)}) collective-permute-start(f32[3,1,1024]{2,1,0:T(1,128)S(1)} %get-tuple-element.34), channel_id=1, source_target_pairs={{4,0},{8,4},{12,8},{16,12},{20,16},{24,20},{28,24},{5,1},{9,5},{13... | collective-permute-start | bytes 36872 | tf_op jit(solution)/shard_map/ppermute | solution.py:184
  3.7 4.5 %collective-permute-start = (f32[3,1,1024]{2,1,0:T(1,128)S(1)}, f32[3,1,1024]{2,1,0:T(1,128)S(1)}, u32[]{:S(2)}, u32[]{:S(2)}) collective-permute-start(f32[3,1,1024]{2,1,0:T(1,128)S(1)} %get-tuple-element.35), channel_id=1, source_target_pairs={{0,4},{4,8},{8,12},{12,16},{16,20},{20,24},{24,28},{1,5},{5,9},{9,... | collective-permute-start | bytes 36872 | tf_op jit(solution)/shard_map/ppermute | solution.py:183
  8.2 1.0 fusion.5
  9.1 1.3 collective-permute-start.3
  10.4 4.0 %collective-permute-start.2 = (f32[3,64,128]{2,1,0:T(8,128)S(1)}, f32[3,64,128]{2,1,0:T(8,128)S(1)}, u32[]{:S(2)}, u32[]{:S(2)}) collective-permute-start(f32[3,64,128]{2,1,0:T(8,128)S(1)} %get-tuple-element.33), channel_id=1, source_target_pairs={{0,1},{1,2},{2,3},{4,5},{5,6},{6,7},{8,9},{9,10},{10,11},{12,13},{... | collective-permute-start | bytes 294920 | tf_op jit(solution)/shard_map/ppermute | solution.py:183
  14.4 1.0 convert_reduce_fusion
  15.4 1.1 slice_reduce_fusion
  16.5 0.7 add_select_fusion
  17.2 0.3 select_reduce_fusion
  17.5 0.7 all_to_all.20
  18.2 4.6 %all-to-all-start = ((s32[32,1,32]{2,1,0:T(1,128)}), s32[32,1,32]{2,1,0:T(1,128)S(1)}, u32[]{:S(2)}, u32[]{:S(2)}) async-start(s32[32,1,32]{2,1,0:T(1,128)} %all_to_all.20), calls=%async_computation | async-start | bytes 32768 | tf_op jit(solution)/shard_map/all_to_all | solution.py:189
  22.8 0.8 copy.39
  23.6 0.1 copy.43
  23.8 0.0 collective-permute-done.1.xhi
  23.8 0.0 collective-permute-done.xlo
  23.8 0.0 collective-permute-done.3.whi
  23.8 0.0 collective-permute-done.2.wlo
  23.8 0.0 copy-done.1
  23.9 0.0 copy-done.3
  23.9 0.7 shard_map.95.one
  24.6 2.2 %collective-permute-start.5 = (f32[3,1,1024]{2,1,0:T(1,128)S(1)}, f32[3,1,1024]{2,1,0:T(1,128)S(1)}, u32[]{:S(2)}, u32[]{:S(2)}) collective-permute-start(f32[3,1,1024]{2,1,0:T(1,128)S(1)} %get-tuple-element.30), channel_id=1, source_target_pairs={{4,0},{8,4},{12,8},{16,12},{20,16},{24,20},{28,24},{5,1},{9,5},{13... | collective-permute-start | bytes 36872 | tf_op jit(solution)/shard_map/ppermute | solution.py:184
  26.8 3.4 %collective-permute-start.4 = (f32[3,1,1024]{2,1,0:T(1,128)S(1)}, f32[3,1,1024]{2,1,0:T(1,128)S(1)}, u32[]{:S(2)}, u32[]{:S(2)}) collective-permute-start(f32[3,1,1024]{2,1,0:T(1,128)S(1)} %get-tuple-element.31), channel_id=1, source_target_pairs={{0,4},{4,8},{8,12},{12,16},{16,20},{20,24},{24,28},{1,5},{5,9},{9,... | collective-permute-start | bytes 36872 | tf_op jit(solution)/shard_map/ppermute | solution.py:183
  30.2 1.3 collective-permute-start.7
  31.5 4.0 %collective-permute-start.6 = (f32[3,64,128]{2,1,0:T(8,128)S(1)}, f32[3,64,128]{2,1,0:T(8,128)S(1)}, u32[]{:S(2)}, u32[]{:S(2)}) collective-permute-start(f32[3,64,128]{2,1,0:T(8,128)S(1)} %get-tuple-element.29), channel_id=1, source_target_pairs={{0,1},{1,2},{2,3},{4,5},{5,6},{6,7},{8,9},{9,10},{10,11},{12,13},{... | collective-permute-start | bytes 294920 | tf_op jit(solution)/shard_map/ppermute | solution.py:183
  35.5 0.7 multiply_add_fusion
  36.2 0.0 all-to-all-done
  36.2 0.5 broadcast.52
  36.7 0.7 reduce.9
  37.4 0.5 broadcast_in_dim_reshape.8.tiles
  38.0 0.0 collective-permute-done.5.xhi
  38.0 0.0 collective-permute-done.4.xlo
  38.0 0.0 collective-permute-done.7.whi
  38.0 0.0 collective-permute-done.6.wlo
  38.0 2.4 %shard_map.96 = (f32[3,64,1024]{2,1,0:T(8,128)S(1)}, f32[1024,384]{1,0:T(8,128)S(1)}) custom-call(f32[3,64,1024]{2,1,0:T(8,128)S(1)} %copy-done.1, f32[3,64,1024]{2,1,0:T(8,128)S(1)} %shard_map.95.one, f32[2,64,1024]{2,1,0:T(8,128)S(1)} %copy-done.3, f32[3,1,1024]{2,1,0:T(1,128)S(1)} %collective-permute-done.4.xlo, ...), custom_call_target="tpu_custom_call" | custom-call | tf_op jit(solution)/shard_map/pallas_call | solution.py:214
  40.4 0.0 copy-start.5
  40.4 1.1 copy-done.5
  41.6 0.9 copy-done.9
  42.4 6.0 %all-to-all-start.1 = ((f32[32,32,384]{2,1,0:T(8,128)}), f32[32,32,384]{2,1,0:T(8,128)S(1)}, u32[]{:S(2)}, u32[]{:S(2)}) async-start(f32[32,32,384]{2,1,0:T(8,128)} %bitcast.11), calls=%async_computation.1 | async-start | bytes 3145728 | tf_op jit(solution)/shard_map/all_to_all | solution.py:189
  48.4 0.0 copy-start.2
  48.5 0.0 copy-start.4
  48.5 1.7 %copy.42.particles = f32[512,3,128]{2,1,0:T(4,128)S(1)} copy(f32[512,3,128]{2,0,1:T(8,128)} %param.10) | data formatting | bytes 1572864 | tf_op args[2]
  50.2 0.0 copy-done.2
  50.2 0.0 copy-done.4
  50.2 24.1 %shard_map.97 = (f32[1024,384]{1,0:T(8,128)S(1)}, f32[1024,384]{1,0:T(8,128)S(1)}) custom-call(s32[1,512]{1,0:T(1,128)S(1)} %add.21.slot_row, s32[512,128]{1,0:T(8,128)S(1)} %copy-done.2, f32[512,3,128]{2,1,0:T(4,128)S(1)} %copy.42.particles, f32[512,2,128]{2,1,0:T(2,128)S(1)} %copy-done.4), custom_call_target="tpu_custom_call" | custom-call | flops 268435456 | bytes 80000000 | tf_op jit(solution)/shard_map/pallas_call | solution.py:221
  74.4 1.2 copy-done.6
  75.5 1.2 copy-done.7
  76.7 9.1 %all-to-all-done.1 = f32[32,32,384]{2,1,0:T(8,128)S(1)} async-done(((f32[32,32,384]{2,1,0:T(8,128)}), f32[32,32,384]{2,1,0:T(8,128)S(1)}, u32[]{:S(2)}, u32[]{:S(2)}) %all-to-all-start.1) | async-done | bytes 1572896 | tf_op jit(solution)/shard_map/all_to_all | solution.py:189
  85.8 3.2 %multiply_subtract_fusion = f32[1024,384]{1,0:T(8,128)} fusion(f32[1024,384]{1,0:T(8,128)} %copy-done.7, f32[1024,384]{1,0:T(8,128)} %copy-done.6, f32[32,32,384]{2,1,0:T(8,128)S(1)} %all-to-all-done.1), kind=kLoop, calls=%fused_computation.2 | loop fusion | flops 786432 | bytes 6291456 | tf_op jit(solution)/shard_map/sub | solution.py:229
  89.0 3.5 %all-to-all-start.2 = ((f32[32,32,384]{2,1,0:T(8,128)}), f32[32,32,384]{2,1,0:T(8,128)}, u32[]{:S(2)}, u32[]{:S(2)}) async-start(f32[32,32,384]{2,1,0:T(8,128)} %bitcast.12), calls=%async_computation.2 | async-start | bytes 3145728 | tf_op jit(solution)/shard_map/all_to_all | solution.py:189
  92.6 0.1 broadcast_in_dim_reshape.7.tiles
  92.7 0.1 copy.44
  92.8 0.1 reshape.67.pairs
  92.9 0.0 copy-start.8
  92.9 13.9 %shard_map.99.acc = f32[512,8,128]{2,1,0:T(8,128)S(1)} custom-call(s32[256]{0:T(256)S(1)} %reshape.67.pairs, f32[512,3,128]{2,1,0:T(4,128)S(1)} %copy.42.particles, s32[128,128,128]{2,1,0:T(8,128)} %contact.1), custom_call_target="tpu_custom_call" | custom-call | flops 67108864 | bytes 25165824 | tf_op jit(solution)/shard_map/pallas_call | solution.py:235
  106.8 1.3 copy-done
  108.2 0.0 copy-done.8
  108.2 5.5 %shard_map.100 = f32[512,3,128]{2,1,0:T(4,128)S(1)} custom-call(f32[1024,384]{1,0:T(8,128)S(1)} %bitcast.10, s32[512,1]{1,0:T(8,128)S(1)} %copy-done.8, s32[512,128]{1,0:T(8,128)S(1)} %copy-done.2, f32[512,3,128]{2,1,0:T(4,128)S(1)} %copy.42.particles, f32[512,2,128]{2,1,0:T(2,128)S(1)} %copy-done.4, f32[512,8,128]{2,1,0:T(8,128)} %copy-done), custom_call_target="tpu_custom_call" | custom-call | flops 805306368 | bytes 10000000 | tf_op jit(solution)/shard_map/pallas_call | solution.py:252
  113.7 0.0 copy-start.10
  113.7 0.9 copy.47
  114.7 15.0 %all-to-all-done.2 = f32[32,32,384]{2,1,0:T(8,128)} async-done(((f32[32,32,384]{2,1,0:T(8,128)}), f32[32,32,384]{2,1,0:T(8,128)}, u32[]{:S(2)}, u32[]{:S(2)}) %all-to-all-start.2) | async-done | bytes 1572896 | tf_op jit(solution)/shard_map/all_to_all | solution.py:189
  129.7 4.1 %shard_map.98 = f32[3,64,1024]{2,1,0:T(8,128)} custom-call(f32[1024,384]{1,0:T(8,128)} %bitcast.5.got, s32[1,1024]{1,0:T(1,128)S(1)} %broadcast_in_dim_reshape.7.tiles, f32[3,64,1024]{2,1,0:T(8,128)S(1)} %copy-done.10), custom_call_target="tpu_custom_call" | custom-call | tf_op jit(solution)/shard_map/pallas_call | solution.py:258
  (10 shorter events, 0.1 us)
Async XLA Ops:
  0.6 23.2 %copy-start.1 = (f32[3,64,1024]{2,1,0:T(8,128)S(1)}, f32[3,64,1024]{2,1,0:T(8,128)}, u32[]{:S(2)}) copy-start(f32[3,64,1024]{2,1,0:T(8,128)} %gas.3) | copy-start | bytes 2359300
  0.6 23.2 %copy-start.3 = (f32[2,64,1024]{2,1,0:T(8,128)S(1)}, f32[2,64,1024]{2,1,0:T(8,128)}, u32[]{:S(2)}) copy-start(f32[2,64,1024]{2,1,0:T(8,128)} %drift.3) | copy-start | bytes 1572868
  1.7 22.1 %collective-permute-start.1 = (f32[3,1,1024]{2,1,0:T(1,128)S(1)}, f32[3,1,1024]{2,1,0:T(1,128)S(1)}, u32[]{:S(2)}, u32[]{:S(2)}) collective-permute-start(f32[3,1,1024]{2,1,0:T(1,128)S(1)} %get-tuple-element.34), channel_id=1, source_target_pairs={{4,0},{8,4},{12,8},{16,12},{20,16},{24,20},{28,24},{5,1},{9,5},{13... | collective-permute-start | bytes 36872 | tf_op jit(solution)/shard_map/ppermute | solution.py:184
  3.7 20.1 %collective-permute-start = (f32[3,1,1024]{2,1,0:T(1,128)S(1)}, f32[3,1,1024]{2,1,0:T(1,128)S(1)}, u32[]{:S(2)}, u32[]{:S(2)}) collective-permute-start(f32[3,1,1024]{2,1,0:T(1,128)S(1)} %get-tuple-element.35), channel_id=1, source_target_pairs={{0,4},{4,8},{8,12},{12,16},{16,20},{20,24},{24,28},{1,5},{5,9},{9,... | collective-permute-start | bytes 36872 | tf_op jit(solution)/shard_map/ppermute | solution.py:183
  9.1 14.7 %collective-permute-start.3 = (f32[3,64,128]{2,1,0:T(8,128)S(1)}, f32[3,64,128]{2,1,0:T(8,128)S(1)}, u32[]{:S(2)}, u32[]{:S(2)}) collective-permute-start(f32[3,64,128]{2,1,0:T(8,128)S(1)} %get-tuple-element.32), channel_id=1, source_target_pairs={{1,0},{2,1},{3,2},{5,4},{6,5},{7,6},{9,8},{10,9},{11,10},{13,12},{... | collective-permute-start | bytes 294920 | tf_op jit(solution)/shard_map/ppermute | solution.py:184
  10.4 13.4 %collective-permute-start.2 = (f32[3,64,128]{2,1,0:T(8,128)S(1)}, f32[3,64,128]{2,1,0:T(8,128)S(1)}, u32[]{:S(2)}, u32[]{:S(2)}) collective-permute-start(f32[3,64,128]{2,1,0:T(8,128)S(1)} %get-tuple-element.33), channel_id=1, source_target_pairs={{0,1},{1,2},{2,3},{4,5},{5,6},{6,7},{8,9},{9,10},{10,11},{12,13},{... | collective-permute-start | bytes 294920 | tf_op jit(solution)/shard_map/ppermute | solution.py:183
  18.2 18.0 %all-to-all-start = ((s32[32,1,32]{2,1,0:T(1,128)}), s32[32,1,32]{2,1,0:T(1,128)S(1)}, u32[]{:S(2)}, u32[]{:S(2)}) async-start(s32[32,1,32]{2,1,0:T(1,128)} %all_to_all.20), calls=%async_computation | async-start | bytes 32768 | tf_op jit(solution)/shard_map/all_to_all | solution.py:189
  24.6 13.4 %collective-permute-start.5 = (f32[3,1,1024]{2,1,0:T(1,128)S(1)}, f32[3,1,1024]{2,1,0:T(1,128)S(1)}, u32[]{:S(2)}, u32[]{:S(2)}) collective-permute-start(f32[3,1,1024]{2,1,0:T(1,128)S(1)} %get-tuple-element.30), channel_id=1, source_target_pairs={{4,0},{8,4},{12,8},{16,12},{20,16},{24,20},{28,24},{5,1},{9,5},{13... | collective-permute-start | bytes 36872 | tf_op jit(solution)/shard_map/ppermute | solution.py:184
  26.8 11.2 %collective-permute-start.4 = (f32[3,1,1024]{2,1,0:T(1,128)S(1)}, f32[3,1,1024]{2,1,0:T(1,128)S(1)}, u32[]{:S(2)}, u32[]{:S(2)}) collective-permute-start(f32[3,1,1024]{2,1,0:T(1,128)S(1)} %get-tuple-element.31), channel_id=1, source_target_pairs={{0,4},{4,8},{8,12},{12,16},{16,20},{20,24},{24,28},{1,5},{5,9},{9,... | collective-permute-start | bytes 36872 | tf_op jit(solution)/shard_map/ppermute | solution.py:183
  30.2 7.8 %collective-permute-start.7 = (f32[3,64,128]{2,1,0:T(8,128)S(1)}, f32[3,64,128]{2,1,0:T(8,128)S(1)}, u32[]{:S(2)}, u32[]{:S(2)}) collective-permute-start(f32[3,64,128]{2,1,0:T(8,128)S(1)} %get-tuple-element.28), channel_id=1, source_target_pairs={{1,0},{2,1},{3,2},{5,4},{6,5},{7,6},{9,8},{10,9},{11,10},{13,12},{... | collective-permute-start | bytes 294920 | tf_op jit(solution)/shard_map/ppermute | solution.py:184
  31.5 6.5 %collective-permute-start.6 = (f32[3,64,128]{2,1,0:T(8,128)S(1)}, f32[3,64,128]{2,1,0:T(8,128)S(1)}, u32[]{:S(2)}, u32[]{:S(2)}) collective-permute-start(f32[3,64,128]{2,1,0:T(8,128)S(1)} %get-tuple-element.29), channel_id=1, source_target_pairs={{0,1},{1,2},{2,3},{4,5},{5,6},{6,7},{8,9},{9,10},{10,11},{12,13},{... | collective-permute-start | bytes 294920 | tf_op jit(solution)/shard_map/ppermute | solution.py:183
  40.4 1.1 copy-start.5
  41.6 0.9 copy-start.9
  42.4 43.4 %all-to-all-start.1 = ((f32[32,32,384]{2,1,0:T(8,128)}), f32[32,32,384]{2,1,0:T(8,128)S(1)}, u32[]{:S(2)}, u32[]{:S(2)}) async-start(f32[32,32,384]{2,1,0:T(8,128)} %bitcast.11), calls=%async_computation.1 | async-start | bytes 3145728 | tf_op jit(solution)/shard_map/all_to_all | solution.py:189
  48.4 1.8 %copy-start.2 = (s32[512,128]{1,0:T(8,128)S(1)}, s32[512,128]{1,0:T(8,128)}, u32[]{:S(2)}) copy-start(s32[512,128]{1,0:T(8,128)} %cells.3) | copy-start | bytes 786436
  48.5 1.8 %copy-start.4 = (f32[512,2,128]{2,1,0:T(2,128)S(1)}, f32[512,2,128]{2,1,0:T(2,128)}, u32[]{:S(2)}) copy-start(f32[512,2,128]{2,1,0:T(2,128)} %rates.3) | copy-start | bytes 1572868
  74.4 1.2 copy-start.6
  75.5 1.2 copy-start.7
  89.0 3.6 %copy-start.11 = (s32[128,2]{0,1:T(2,128)S(1)}, s32[128,2]{0,1:T(2,128)}, u32[]{:S(2)}) copy-start(s32[128,2]{0,1:T(2,128)} %param.14) | copy-start | bytes 3076
  89.0 40.6 %all-to-all-start.2 = ((f32[32,32,384]{2,1,0:T(8,128)}), f32[32,32,384]{2,1,0:T(8,128)}, u32[]{:S(2)}, u32[]{:S(2)}) async-start(f32[32,32,384]{2,1,0:T(8,128)} %bitcast.12), calls=%async_computation.2 | async-start | bytes 3145728 | tf_op jit(solution)/shard_map/all_to_all | solution.py:189
  92.9 15.3 %copy-start.8 = (s32[512,1]{1,0:T(8,128)S(1)}, s32[512,1]{1,0:T(8,128)}, u32[]{:S(2)}) copy-start(s32[512,1]{1,0:T(8,128)} %get-tuple-element.36.slot_col) | copy-start | bytes 6148
  106.8 1.3 %copy-start = (f32[512,8,128]{2,1,0:T(8,128)}, f32[512,8,128]{2,1,0:T(8,128)S(1)}, u32[]{:S(2)}) copy-start(f32[512,8,128]{2,1,0:T(8,128)S(1)} %shard_map.99.acc) | copy-start | bytes 6291460
  113.7 15.9 %copy-start.10 = (f32[3,64,1024]{2,1,0:T(8,128)S(1)}, f32[3,64,1024]{2,1,0:T(8,128)}, u32[]{:S(2)}) copy-start(f32[3,64,1024]{2,1,0:T(8,128)} %copy-done.9) | copy-start | bytes 2359300

commit v3 on v2

--- a/solution.py
+++ b/solution.py
@@ -43,27 +43,71 @@
     return VISCOSITY * (west + east + south + north - 4.0 * v) - upwind
 
 
-def halo_terms(k, v, xlo, xhi, wlo, whi, drift):
-    return tendency(
-        v, xlo[k], xhi[k], wlo[k, :, LANES - 1 : LANES], whi[k, :, 0:1], drift[0], drift[1]
-    )
-
-
-def first_kernel(gas, drift, xlo, xhi, wlo, whi, out):
-    for k in range(3):
-        v = gas[k]
-        out[k] = v + TIME_STEP * halo_terms(k, v, xlo, xhi, wlo, whi, drift)
-
-
-def second_kernel(gas, one, drift, xlo, xhi, wlo, whi, tiles, out, sent, table):
+def transport_kernel(gas, drift, out, table, one, rows_in, cols_in, send, recv):
     _, rows, cols = gas.shape
     per_row = cols // LANES
+    x, w = lax.axis_index("slab"), lax.axis_index("pblk")
+    nx, nw = lax.axis_size("slab"), lax.axis_size("pblk")
+    places = (
+        (lax.rem(x + 1, nx), w),
+        (lax.rem(x + nx - 1, nx), w),
+        (x, lax.rem(w + 1, nw)),
+        (x, lax.rem(w + nw - 1, nw)),
+    )
+    barrier = pltpu.get_barrier_semaphore()
+    for place in places:
+        pl.semaphore_signal(
+            barrier, inc=1, device_id=place, device_id_type=pl.DeviceIdType.MESH
+        )
+    pl.semaphore_wait(barrier, 4)
+
+    def trade(v, turn):
+        edges = (
+            (v.at[:, pl.ds(rows - 8, 8), :], rows_in.at[2 * turn]),
+            (v.at[:, pl.ds(0, 8), :], rows_in.at[2 * turn + 1]),
+            (v.at[:, :, pl.ds(cols - LANES, LANES)], cols_in.at[2 * turn]),
+            (v.at[:, :, pl.ds(0, LANES)], cols_in.at[2 * turn + 1]),
+        )
+        copies = [
+            pltpu.make_async_remote_copy(
+                src_ref=src,
+                dst_ref=dst,
+                send_sem=send.at[4 * turn + n],
+                recv_sem=recv.at[4 * turn + n],
+                device_id=places[n],
+                device_id_type=pl.DeviceIdType.MESH,
+            )
+            for n, (src, dst) in enumerate(edges)
+        ]
+        for copy in copies:
+            copy.start()
+        return copies
+
+    def stencil(v, k, turn):
+        xlo = jnp.where(x == 0, 0.0, rows_in[2 * turn, k, 7:8, :])
+        xhi = jnp.where(x == nx - 1, 0.0, rows_in[2 * turn + 1, k, 0:1, :])
+        wlo = jnp.where(w == 0, 0.0, cols_in[2 * turn, k][:, LANES - 1 : LANES])
+        whi = jnp.where(w == nw - 1, 0.0, cols_in[2 * turn + 1, k][:, 0:1])
+        return tendency(v, xlo, xhi, wlo, whi, drift[0], drift[1])
+
+    copies = trade(gas, 0)
+    for copy in copies:
+        copy.wait()
+    for k in range(3):
+        v = gas[k]
+        one[k] = v + TIME_STEP * stencil(v, k, 0)
+    copies = trade(one, 1)
+    for copy in copies:
+        copy.wait()
     for k in range(3):
         v = one[k]
-        two = 0.5 * (gas[k] + v + TIME_STEP * halo_terms(k, v, xlo, xhi, wlo, whi, drift))
+        two = 0.5 * (gas[k] + v + TIME_STEP * stencil(v, k, 1))
         out[k] = two
         for j in range(per_row):
             table[k, pl.ds(j, rows, stride=per_row), :] = two[:, j * LANES : (j + 1) * LANES]
+
+
+def gather_kernel(table, tiles, sent):
     count = table.shape[1]
     slots = tiles.shape[0]
     one_hot = (
@@ -71,6 +115,10 @@
     ).astype(F32).astype(BF)
     for k in range(3):
         sent[:, k * LANES : (k + 1) * LANES] = select_rows(one_hot, table[k])
+
+
+def combine_kernel(got, rate_sums, state_sums, sent):
+    sent[...] = got[...] * rate_sums[...] - state_sums[...]
 
 
 def contact_kernel(pairs, particles, contact, acc, parts):
@@ -171,18 +219,6 @@
 
 def cost(flops, moved):
     return pl.CostEstimate(flops=flops, bytes_accessed=moved, transcendentals=0)
-
-
-def halos(v):
-    found = []
-    for axis, dim, width in (("slab", 1, 1), ("pblk", 2, LANES)):
-        count = lax.axis_size(axis)
-        up = [(i, i + 1) for i in range(count - 1)]
-        down = [(i + 1, i) for i in range(count - 1)]
-        size = v.shape[dim]
-        found.append(lax.ppermute(lax.slice_in_dim(v, size - width, size, axis=dim), axis, up))
-        found.append(lax.ppermute(lax.slice_in_dim(v, 0, width, axis=dim), axis, down))
-    return found
 
 
 def exchange(x):
@@ -208,15 +244,27 @@
 
     field = jax.ShapeDtypeStruct(gas.shape, F32)
     wide = jax.ShapeDtypeStruct((slots, 3 * LANES), F32)
-    one = pl.pallas_call(first_kernel, out_shape=field, compiler_params=params())(
-        gas, drift, *halos(gas)
-    )
-    two, sent_gas = pl.pallas_call(
-        second_kernel,
-        out_shape=(field, wide),
-        scratch_shapes=[pltpu.VMEM((3, tile_count, LANES), F32)],
-        compiler_params=params(),
-    )(gas, one, drift, *halos(one), tiles[:, None])
+    rows, cols = gas.shape[1:]
+    two, table = pl.pallas_call(
+        transport_kernel,
+        out_shape=(field, jax.ShapeDtypeStruct((3, tile_count, LANES), F32)),
+        in_specs=[pl.BlockSpec(memory_space=pltpu.VMEM)] * 2,
+        out_specs=(pl.BlockSpec(memory_space=pltpu.VMEM),) * 2,
+        scratch_shapes=[
+            pltpu.VMEM((3, rows, cols), F32),
+            pltpu.VMEM((4, 3, 8, cols), F32),
+            pltpu.VMEM((4, 3, rows, LANES), F32),
+            pltpu.SemaphoreType.DMA((8,)),
+            pltpu.SemaphoreType.DMA((8,)),
+        ],
+        compiler_params=pltpu.CompilerParams(
+            collective_id=0, has_side_effects=True, vmem_limit_bytes=VMEM_BYTES
+        ),
+        cost_estimate=cost(3 * 40 * rows * cols, 30_000_000),
+    )(gas, drift)
+    sent_gas = pl.pallas_call(gather_kernel, out_shape=wide, compiler_params=params())(
+        table, tiles[:, None]
+    )
     slot_row, sent_gas = lax.optimization_barrier((slot[None, :], sent_gas))
     rate_sums, state_sums = pl.pallas_call(
         sums_kernel,
@@ -226,7 +274,9 @@
         cost_estimate=cost(blocks * 32 * LANES * LANES, 80_000_000),
     )(slot_row, cells, particles, rates)
     got_gas = exchange(sent_gas)
-    sent_terms = got_gas * rate_sums - state_sums
+    sent_terms = pl.pallas_call(combine_kernel, out_shape=wide, compiler_params=params())(
+        got_gas, rate_sums, state_sums
+    )
     pairs, sent_terms = lax.optimization_barrier((pairs, sent_terms))
     got_terms = exchange(sent_terms)
 

time: 135 us -> 128 us (0.948)
  starting transfers between devices: 36.7 us -> 16.9 us
  Pallas kernels: 50.8 us -> 67.2 us
  other arithmetic: 6.66 us -> 3.49 us
    ppermute x8 -> x0, starting transfers between devices: 22.6 us -> none  [the longest x4 15.8 us: halos(): lax.ppermute(lax.slice_in_dim(v, size - width, size, axis=dim), axis, up)]
    pallas_call x2 -> x3, Pallas kernels: 3.08 us -> 19.5 us  [the longest x1 14.9 us: on_device(): pl.pallas_call(transport_kernel, out_shape=(field, jax.ShapeDtypeStruct((...]
    sub x1 -> x0, other arithmetic: 3.23 us -> none  [on_device(): sent_terms = got_gas * rate_sums - state_sums]
    all_to_all x3, starting transfers between devices: 14.1 us -> 16.9 us  [exchange(): lax.all_to_all(x, ('slab', 'pblk'), split_axis=0, concat_axis=0, tiled=True)]
    unnamed x27 -> x29, local copies, waits for them, and re-layouts: 9.21 us -> 11.6 us
    slice x4 -> x0, local copies, waits for them, and re-layouts: 2.06 us -> none  [halos(): lax.slice_in_dim(v, 0, width, axis=dim)]
  transfers between devices with their start and end apart: 11 -> 3, of which waited for: 2 -> 2; matrix products, arithmetic and copies ran while one was open for 8% -> 4% of each run, Pallas kernels for 33% -> 46%
where the time goes in v3:
time: 128 us
  Pallas kernels  67.2 us (52%)
  waiting for transfers between devices  24.2 us (19%)
  starting transfers between devices  16.9 us (13%)
  local copies, waits for them, and re-layouts  14.9 us (12%)
  other arithmetic  3.49 us (3%)
    all_to_all x3, waiting for transfers between devices, exchange(): lax.all_to_all(x, ('slab', 'pblk'), split_axis=0, concat_axis=0, tiled=True)  24.2 us
    pallas_call x1, Pallas kernels, on_device(): pl.pallas_call(sums_kernel, out_shape=(wide, wide), scratch_shapes=[pltpu...  24.1 us
    all_to_all x3, starting transfers between devices, exchange(): lax.all_to_all(x, ('slab', 'pblk'), split_axis=0, concat_axis=0, tiled=True)  16.9 us
    pallas_call x1, Pallas kernels, on_device(): pl.pallas_call(transport_kernel, out_shape=(field, jax.ShapeDtypeStruct((...  14.9 us
    pallas_call x1, Pallas kernels, on_device(): pl.pallas_call(contact_kernel, grid_spec=pltpu.PrefetchScalarGridSpec(num...  13.9 us
    unnamed x29, local copies, waits for them, and re-layouts  11.6 us
    pallas_call x1, Pallas kernels, on_device(): pl.pallas_call(particles_kernel, out_shape=jax.ShapeDtypeStruct(particles...  5.54 us
    pallas_call x1, Pallas kernels, on_device(): pl.pallas_call(sources_kernel, out_shape=field, scratch_shapes=[pltpu.VME...  4.13 us
  transfers between devices with their start and end apart: 3, of which 2 were waited for; matrix products, arithmetic and copies ran while one was open for 4% of the time, Pallas kernels for 46%

profile of v3, /device:TPU:1, one launch (start us, length us, event | category | flops | bytes accessed | tf_op | source)
XLA Modules:
  0.0 127.5 jit_solution(1414636362497192753)
XLA Ops:
  0.6 0.0 copy-start.8
  0.6 1.0 convert_reduce_fusion
  1.7 1.1 slice_reduce_fusion
  2.8 0.7 add_select_fusion
  3.5 0.3 select_reduce_fusion
  3.7 0.7 all_to_all.20
  4.4 7.1 %all-to-all-start = ((s32[32,1,32]{2,1,0:T(1,128)}), s32[32,1,32]{2,1,0:T(1,128)S(1)}, u32[]{:S(2)}, u32[]{:S(2)}) async-start(s32[32,1,32]{2,1,0:T(1,128)} %all_to_all.20), calls=%async_computation | async-start | bytes 32768 | tf_op jit(solution)/shard_map/all_to_all | solution.py:225
  11.5 0.8 copy.39
  12.4 0.1 copy.43
  12.5 0.7 multiply_add_fusion
  13.3 0.0 copy-done.8
  13.3 0.0 copy-start.11
  13.3 1.0 copy-done.11
  14.3 14.9 %shard_map.95 = (f32[3,64,1024]{2,1,0:T(8,128)S(1)}, f32[3,512,128]{2,1,0:T(8,128)S(1)}) custom-call(f32[3,64,1024]{2,1,0:T(8,128)S(1)} %copy-done.8, f32[2,64,1024]{2,1,0:T(8,128)S(1)} %copy-done.11), custom_call_target="tpu_custom_call" | custom-call | flops 7864320 | bytes 30000000 | tf_op jit(solution)/shard_map/pallas_call | solution.py:248
  29.2 0.0 copy-start.9
  29.2 0.9 copy-done.9
  30.1 0.0 all-to-all-done
  30.1 0.6 broadcast.52
  30.7 0.7 reduce.9
  31.4 0.5 broadcast_in_dim_reshape.8.tiles
  31.9 3.0 %shard_map.96 = f32[1024,384]{1,0:T(8,128)} custom-call(f32[3,512,128]{2,1,0:T(8,128)S(1)} %get-tuple-element.10.table, s32[1024,1]{1,0:T(8,128)S(1)} %broadcast_in_dim_reshape.8.tiles), custom_call_target="tpu_custom_call" | custom-call | tf_op jit(solution)/shard_map/pallas_call | solution.py:265
  34.9 0.0 copy-start.2
  34.9 0.0 copy-start.3
  34.9 6.3 %all-to-all-start.1 = ((f32[32,32,384]{2,1,0:T(8,128)}), f32[32,32,384]{2,1,0:T(8,128)S(1)}, u32[]{:S(2)}, u32[]{:S(2)}) async-start(f32[32,32,384]{2,1,0:T(8,128)} %bitcast.2), calls=%async_computation.1 | async-start | bytes 3145728 | tf_op jit(solution)/shard_map/all_to_all | solution.py:225
  41.2 1.7 %copy.42.particles = f32[512,3,128]{2,1,0:T(4,128)S(1)} copy(f32[512,3,128]{2,0,1:T(8,128)} %param.10) | data formatting | bytes 1572864 | tf_op args[2]
  42.9 0.0 copy-done.2
  42.9 0.0 copy-done.3
  42.9 24.1 %shard_map.97 = (f32[1024,384]{1,0:T(8,128)S(1)}, f32[1024,384]{1,0:T(8,128)S(1)}) custom-call(s32[1,512]{1,0:T(1,128)S(1)} %add.21.slot_row, s32[512,128]{1,0:T(8,128)S(1)} %copy-done.2, f32[512,3,128]{2,1,0:T(4,128)S(1)} %copy.42.particles, f32[512,2,128]{2,1,0:T(2,128)S(1)} %copy-done.3), custom_call_target="tpu_custom_call" | custom-call | flops 268435456 | bytes 80000000 | tf_op jit(solution)/shard_map/pallas_call | solution.py:269
  67.1 0.0 copy-start.4
  67.1 1.1 copy-done.4
  68.2 0.0 copy-start.6
  68.2 1.2 copy-done.6
  69.4 9.2 %all-to-all-done.1 = f32[32,32,384]{2,1,0:T(8,128)S(1)} async-done(((f32[32,32,384]{2,1,0:T(8,128)}), f32[32,32,384]{2,1,0:T(8,128)S(1)}, u32[]{:S(2)}, u32[]{:S(2)}) %all-to-all-start.1) | async-done | bytes 1572896 | tf_op jit(solution)/shard_map/all_to_all | solution.py:225
  78.6 0.0 copy-start.5
  78.6 1.4 %copy-done.5 = f32[1024,384]{1,0:T(8,128)S(1)} copy-done((f32[1024,384]{1,0:T(8,128)S(1)}, f32[1024,384]{1,0:T(8,128)}, u32[]{:S(2)}) %copy-start.5) | copy-done | bytes 1572888
  80.0 1.6 %shard_map.98 = f32[1024,384]{1,0:T(8,128)S(1)} custom-call(f32[1024,384]{1,0:T(8,128)S(1)} %bitcast.9, f32[1024,384]{1,0:T(8,128)S(1)} %copy-done.5, f32[1024,384]{1,0:T(8,128)} %copy-done.6), custom_call_target="tpu_custom_call" | custom-call | tf_op jit(solution)/shard_map/pallas_call | solution.py:277
  81.6 0.0 copy-start.1
  81.6 1.1 copy-done.1
  82.7 0.0 copy-start.12
  82.7 3.5 %all-to-all-start.2 = ((f32[32,32,384]{2,1,0:T(8,128)}), f32[32,32,384]{2,1,0:T(8,128)}, u32[]{:S(2)}, u32[]{:S(2)}) async-start(f32[32,32,384]{2,1,0:T(8,128)} %bitcast.11), calls=%async_computation.2 | async-start | bytes 3145728 | tf_op jit(solution)/shard_map/all_to_all | solution.py:225
  86.3 0.1 broadcast_in_dim_reshape.7.tiles
  86.3 0.0 copy-done.12
  86.3 0.1 copy.44
  86.5 0.1 reshape.67.pairs
  86.6 0.0 copy-start.7
  86.6 13.9 %shard_map.100.acc = f32[512,8,128]{2,1,0:T(8,128)S(1)} custom-call(s32[256]{0:T(256)S(1)} %reshape.67.pairs, f32[512,3,128]{2,1,0:T(4,128)S(1)} %copy.42.particles, s32[128,128,128]{2,1,0:T(8,128)} %contact.1), custom_call_target="tpu_custom_call" | custom-call | flops 67108864 | bytes 25165824 | tf_op jit(solution)/shard_map/pallas_call | solution.py:285
  100.5 0.0 copy-start
  100.5 1.3 %copy-done = f32[512,8,128]{2,1,0:T(8,128)} copy-done((f32[512,8,128]{2,1,0:T(8,128)}, f32[512,8,128]{2,1,0:T(8,128)S(1)}, u32[]{:S(2)}) %copy-start) | copy-done | bytes 2097176
  101.9 0.0 copy-done.7
  101.9 5.5 %shard_map.101 = f32[512,3,128]{2,1,0:T(4,128)S(1)} custom-call(f32[1024,384]{1,0:T(8,128)S(1)} %bitcast.10, s32[512,1]{1,0:T(8,128)S(1)} %copy-done.7, s32[512,128]{1,0:T(8,128)S(1)} %copy-done.2, f32[512,3,128]{2,1,0:T(4,128)S(1)} %copy.42.particles, f32[512,2,128]{2,1,0:T(2,128)S(1)} %copy-done.3, f32[512,8,128]{2,1,0:T(8,128)} %copy-done), custom_call_target="tpu_custom_call" | custom-call | flops 805306368 | bytes 10000000 | tf_op jit(solution)/shard_map/pallas_call | solution.py:302
  107.4 0.0 copy-start.10
  107.4 0.9 copy.47
  108.4 15.0 %all-to-all-done.2 = f32[32,32,384]{2,1,0:T(8,128)} async-done(((f32[32,32,384]{2,1,0:T(8,128)}), f32[32,32,384]{2,1,0:T(8,128)}, u32[]{:S(2)}, u32[]{:S(2)}) %all-to-all-start.2) | async-done | bytes 1572896 | tf_op jit(solution)/shard_map/all_to_all | solution.py:225
  123.4 0.0 copy-done.10
  123.4 4.1 %shard_map.99 = f32[3,64,1024]{2,1,0:T(8,128)} custom-call(f32[1024,384]{1,0:T(8,128)} %bitcast.5.got, s32[1,1024]{1,0:T(1,128)S(1)} %broadcast_in_dim_reshape.7.tiles, f32[3,64,1024]{2,1,0:T(8,128)S(1)} %copy-done.10), custom_call_target="tpu_custom_call" | custom-call | tf_op jit(solution)/shard_map/pallas_call | solution.py:308
  (1 shorter events, 0.0 us)
Async XLA Ops:
  0.6 12.7 %copy-start.8 = (f32[3,64,1024]{2,1,0:T(8,128)S(1)}, f32[3,64,1024]{2,1,0:T(8,128)}, u32[]{:S(2)}) copy-start(f32[3,64,1024]{2,1,0:T(8,128)} %gas.1) | copy-start | bytes 2359300
  4.4 25.6 %all-to-all-start = ((s32[32,1,32]{2,1,0:T(1,128)}), s32[32,1,32]{2,1,0:T(1,128)S(1)}, u32[]{:S(2)}, u32[]{:S(2)}) async-start(s32[32,1,32]{2,1,0:T(1,128)} %all_to_all.20), calls=%async_computation | async-start | bytes 32768 | tf_op jit(solution)/shard_map/all_to_all | solution.py:225
  13.3 1.0 copy-start.11
  29.2 0.9 copy-start.9
  34.9 8.0 %copy-start.2 = (s32[512,128]{1,0:T(8,128)S(1)}, s32[512,128]{1,0:T(8,128)}, u32[]{:S(2)}) copy-start(s32[512,128]{1,0:T(8,128)} %cells.3) | copy-start | bytes 786436
  34.9 8.0 %copy-start.3 = (f32[512,2,128]{2,1,0:T(2,128)S(1)}, f32[512,2,128]{2,1,0:T(2,128)}, u32[]{:S(2)}) copy-start(f32[512,2,128]{2,1,0:T(2,128)} %rates.3) | copy-start | bytes 1572868
  34.9 43.6 %all-to-all-start.1 = ((f32[32,32,384]{2,1,0:T(8,128)}), f32[32,32,384]{2,1,0:T(8,128)S(1)}, u32[]{:S(2)}, u32[]{:S(2)}) async-start(f32[32,32,384]{2,1,0:T(8,128)} %bitcast.2), calls=%async_computation.1 | async-start | bytes 3145728 | tf_op jit(solution)/shard_map/all_to_all | solution.py:225
  67.1 1.2 copy-start.4
  68.2 1.2 copy-start.6
  78.6 1.4 %copy-start.5 = (f32[1024,384]{1,0:T(8,128)S(1)}, f32[1024,384]{1,0:T(8,128)}, u32[]{:S(2)}) copy-start(f32[1024,384]{1,0:T(8,128)} %copy-done.4) | copy-start | bytes 4718596
  81.6 1.1 copy-start.1
  82.7 3.6 %copy-start.12 = (s32[128,2]{0,1:T(2,128)S(1)}, s32[128,2]{0,1:T(2,128)}, u32[]{:S(2)}) copy-start(s32[128,2]{0,1:T(2,128)} %param.14) | copy-start | bytes 3076
  82.7 40.6 %all-to-all-start.2 = ((f32[32,32,384]{2,1,0:T(8,128)}), f32[32,32,384]{2,1,0:T(8,128)}, u32[]{:S(2)}, u32[]{:S(2)}) async-start(f32[32,32,384]{2,1,0:T(8,128)} %bitcast.11), calls=%async_computation.2 | async-start | bytes 3145728 | tf_op jit(solution)/shard_map/all_to_all | solution.py:225
  86.6 15.3 %copy-start.7 = (s32[512,1]{1,0:T(8,128)S(1)}, s32[512,1]{1,0:T(8,128)}, u32[]{:S(2)}) copy-start(s32[512,1]{1,0:T(8,128)} %get-tuple-element.28.slot_col) | copy-start | bytes 6148
  100.5 1.3 %copy-start = (f32[512,8,128]{2,1,0:T(8,128)}, f32[512,8,128]{2,1,0:T(8,128)S(1)}, u32[]{:S(2)}) copy-start(f32[512,8,128]{2,1,0:T(8,128)S(1)} %shard_map.100.acc) | copy-start | bytes 6291460
  107.4 15.9 %copy-start.10 = (f32[3,64,1024]{2,1,0:T(8,128)S(1)}, f32[3,64,1024]{2,1,0:T(8,128)}, u32[]{:S(2)}) copy-start(f32[3,64,1024]{2,1,0:T(8,128)} %copy-done.9) | copy-start | bytes 2359300

commit v4 on v3

--- a/solution.py
+++ b/solution.py
@@ -43,7 +43,9 @@
     return VISCOSITY * (west + east + south + north - 4.0 * v) - upwind
 
 
-def transport_kernel(gas, drift, out, table, one, rows_in, cols_in, send, recv):
+def transport_kernel(
+    gas, drift, out, table, one, rows_out, cols_out, rows_in, cols_in, send, recv
+):
     _, rows, cols = gas.shape
     per_row = cols // LANES
     x, w = lax.axis_index("slab"), lax.axis_index("pblk")
@@ -59,14 +61,26 @@
         pl.semaphore_signal(
             barrier, inc=1, device_id=place, device_id_type=pl.DeviceIdType.MESH
         )
+    rows_out[...] = jnp.zeros_like(rows_out)
+    cols_out[...] = jnp.zeros_like(cols_out)
+
+    def pack(v, k, turn):
+        rows_out[2 * turn, k : k + 1, :] = v[rows - 1 : rows, :]
+        rows_out[2 * turn + 1, k : k + 1, :] = v[0:1, :]
+        cols_out[2 * turn, :, k : k + 1] = v[:, cols - 1 : cols]
+        cols_out[2 * turn + 1, :, k : k + 1] = v[:, 0:1]
+
+    for k in range(3):
+        pack(gas[k], k, 0)
     pl.semaphore_wait(barrier, 4)
 
-    def trade(v, turn):
+    def trade(turn):
+        low, high = 2 * turn, 2 * turn + 1
         edges = (
-            (v.at[:, pl.ds(rows - 8, 8), :], rows_in.at[2 * turn]),
-            (v.at[:, pl.ds(0, 8), :], rows_in.at[2 * turn + 1]),
-            (v.at[:, :, pl.ds(cols - LANES, LANES)], cols_in.at[2 * turn]),
-            (v.at[:, :, pl.ds(0, LANES)], cols_in.at[2 * turn + 1]),
+            (rows_out.at[low], rows_in.at[low]),
+            (rows_out.at[high], rows_in.at[high]),
+            (cols_out.at[low], cols_in.at[low]),
+            (cols_out.at[high], cols_in.at[high]),
         )
         copies = [
             pltpu.make_async_remote_copy(
@@ -84,19 +98,22 @@
         return copies
 
     def stencil(v, k, turn):
-        xlo = jnp.where(x == 0, 0.0, rows_in[2 * turn, k, 7:8, :])
-        xhi = jnp.where(x == nx - 1, 0.0, rows_in[2 * turn + 1, k, 0:1, :])
-        wlo = jnp.where(w == 0, 0.0, cols_in[2 * turn, k][:, LANES - 1 : LANES])
-        whi = jnp.where(w == nw - 1, 0.0, cols_in[2 * turn + 1, k][:, 0:1])
+        low, high = 2 * turn, 2 * turn + 1
+        xlo = jnp.where(x == 0, 0.0, rows_in[low, k : k + 1, :])
+        xhi = jnp.where(x == nx - 1, 0.0, rows_in[high, k : k + 1, :])
+        wlo = jnp.where(w == 0, 0.0, cols_in[low][:, k : k + 1])
+        whi = jnp.where(w == nw - 1, 0.0, cols_in[high][:, k : k + 1])
         return tendency(v, xlo, xhi, wlo, whi, drift[0], drift[1])
 
-    copies = trade(gas, 0)
+    copies = trade(0)
     for copy in copies:
         copy.wait()
     for k in range(3):
         v = gas[k]
-        one[k] = v + TIME_STEP * stencil(v, k, 0)
-    copies = trade(one, 1)
+        first = v + TIME_STEP * stencil(v, k, 0)
+        one[k] = first
+        pack(first, k, 1)
+    copies = trade(1)
     for copy in copies:
         copy.wait()
     for k in range(3):
@@ -252,8 +269,10 @@
         out_specs=(pl.BlockSpec(memory_space=pltpu.VMEM),) * 2,
         scratch_shapes=[
             pltpu.VMEM((3, rows, cols), F32),
-            pltpu.VMEM((4, 3, 8, cols), F32),
-            pltpu.VMEM((4, 3, rows, LANES), F32),
+            pltpu.VMEM((4, 8, cols), F32),
+            pltpu.VMEM((4, rows, LANES), F32),
+            pltpu.VMEM((4, 8, cols), F32),
+            pltpu.VMEM((4, rows, LANES), F32),
             pltpu.SemaphoreType.DMA((8,)),
             pltpu.SemaphoreType.DMA((8,)),
         ],

time: 128 us -> 124 us (0.969)
  Pallas kernels: 67.2 us -> 63.6 us
    pallas_call x1, Pallas kernels: 14.9 us -> 11.3 us  [on_device(): pl.pallas_call(transport_kernel, out_shape=(field, jax.ShapeDtypeStruct((...]
  transfers between devices with their start and end apart: 3 -> 3, of which waited for: 2 -> 2; matrix products, arithmetic and copies ran while one was open for 4% -> 4% of each run, Pallas kernels for 46% -> 45%
where the time goes in v4:
time: 124 us; the launch traced here: 123 us
  Pallas kernels  63.6 us (51%)
  waiting for transfers between devices  24.2 us (20%)
  starting transfers between devices  15.8 us (13%)
  local copies, waits for them, and re-layouts  14.9 us (12%)
  other arithmetic  3.49 us (3%)
    all_to_all x3, waiting for transfers between devices, exchange(): lax.all_to_all(x, ('slab', 'pblk'), split_axis=0, concat_axis=0, tiled=True)  24.2 us
    pallas_call x1, Pallas kernels, on_device(): pl.pallas_call(sums_kernel, out_shape=(wide, wide), scratch_shapes=[pltpu...  24.1 us
    all_to_all x3, starting transfers between devices, exchange(): lax.all_to_all(x, ('slab', 'pblk'), split_axis=0, concat_axis=0, tiled=True)  15.8 us
    pallas_call x1, Pallas kernels, on_device(): pl.pallas_call(contact_kernel, grid_spec=pltpu.PrefetchScalarGridSpec(num...  13.9 us
    unnamed x29, local copies, waits for them, and re-layouts  11.6 us
    pallas_call x1, Pallas kernels, on_device(): pl.pallas_call(transport_kernel, out_shape=(field, jax.ShapeDtypeStruct((...  11.3 us
    pallas_call x1, Pallas kernels, on_device(): pl.pallas_call(particles_kernel, out_shape=jax.ShapeDtypeStruct(particles...  5.55 us
    pallas_call x1, Pallas kernels, on_device(): pl.pallas_call(sources_kernel, out_shape=field, scratch_shapes=[pltpu.VME...  4.13 us
  transfers between devices with their start and end apart: 3, of which 2 were waited for; matrix products, arithmetic and copies ran while one was open for 4% of the time, Pallas kernels for 45%

profile of v4, /device:TPU:1, one launch (start us, length us, event | category | flops | bytes accessed | tf_op | source)
XLA Modules:
  0.0 122.8 jit_solution(8458115060323805888)
XLA Ops:
  0.6 0.0 copy-start.8
  0.6 1.0 convert_reduce_fusion
  1.7 1.1 slice_reduce_fusion
  2.8 0.7 add_select_fusion
  3.5 0.3 select_reduce_fusion
  3.7 0.7 all_to_all.20
  4.4 7.1 %all-to-all-start = ((s32[32,1,32]{2,1,0:T(1,128)}), s32[32,1,32]{2,1,0:T(1,128)S(1)}, u32[]{:S(2)}, u32[]{:S(2)}) async-start(s32[32,1,32]{2,1,0:T(1,128)} %all_to_all.20), calls=%async_computation | async-start | bytes 32768 | tf_op jit(solution)/shard_map/all_to_all | solution.py:242
  11.5 0.8 copy.39
  12.4 0.1 copy.43
  12.5 0.7 multiply_add_fusion
  13.3 0.0 copy-done.8
  13.3 0.0 copy-start.11
  13.3 1.0 copy-done.11
  14.3 11.3 %shard_map.95 = (f32[3,64,1024]{2,1,0:T(8,128)S(1)}, f32[3,512,128]{2,1,0:T(8,128)S(1)}) custom-call(f32[3,64,1024]{2,1,0:T(8,128)S(1)} %copy-done.8, f32[2,64,1024]{2,1,0:T(8,128)S(1)} %copy-done.11), custom_call_target="tpu_custom_call" | custom-call | flops 7864320 | bytes 30000000 | tf_op jit(solution)/shard_map/pallas_call | solution.py:265
  25.6 0.0 copy-start.9
  25.6 0.9 copy-done.9
  26.5 0.0 all-to-all-done
  26.5 0.6 broadcast.52
  27.1 0.7 reduce.9
  27.8 0.5 broadcast_in_dim_reshape.8.tiles
  28.3 3.0 %shard_map.96 = f32[1024,384]{1,0:T(8,128)} custom-call(f32[3,512,128]{2,1,0:T(8,128)S(1)} %get-tuple-element.10.table, s32[1024,1]{1,0:T(8,128)S(1)} %broadcast_in_dim_reshape.8.tiles), custom_call_target="tpu_custom_call" | custom-call | tf_op jit(solution)/shard_map/pallas_call | solution.py:284
  31.4 0.0 copy-start.2
  31.4 0.0 copy-start.3
  31.4 5.2 %all-to-all-start.1 = ((f32[32,32,384]{2,1,0:T(8,128)}), f32[32,32,384]{2,1,0:T(8,128)S(1)}, u32[]{:S(2)}, u32[]{:S(2)}) async-start(f32[32,32,384]{2,1,0:T(8,128)} %bitcast.2), calls=%async_computation.1 | async-start | bytes 3145728 | tf_op jit(solution)/shard_map/all_to_all | solution.py:242
  36.5 1.7 %copy.42.particles = f32[512,3,128]{2,1,0:T(4,128)S(1)} copy(f32[512,3,128]{2,0,1:T(8,128)} %param.10) | data formatting | bytes 1572864 | tf_op args[2]
  38.2 0.0 copy-done.2
  38.2 0.0 copy-done.3
  38.2 24.1 %shard_map.97 = (f32[1024,384]{1,0:T(8,128)S(1)}, f32[1024,384]{1,0:T(8,128)S(1)}) custom-call(s32[1,512]{1,0:T(1,128)S(1)} %add.21.slot_row, s32[512,128]{1,0:T(8,128)S(1)} %copy-done.2, f32[512,3,128]{2,1,0:T(4,128)S(1)} %copy.42.particles, f32[512,2,128]{2,1,0:T(2,128)S(1)} %copy-done.3), custom_call_target="tpu_custom_call" | custom-call | flops 268435456 | bytes 80000000 | tf_op jit(solution)/shard_map/pallas_call | solution.py:288
  62.4 0.0 copy-start.4
  62.4 1.1 copy-done.4
  63.5 0.0 copy-start.6
  63.5 1.2 copy-done.6
  64.7 9.2 %all-to-all-done.1 = f32[32,32,384]{2,1,0:T(8,128)S(1)} async-done(((f32[32,32,384]{2,1,0:T(8,128)}), f32[32,32,384]{2,1,0:T(8,128)S(1)}, u32[]{:S(2)}, u32[]{:S(2)}) %all-to-all-start.1) | async-done | bytes 1572896 | tf_op jit(solution)/shard_map/all_to_all | solution.py:242
  73.9 0.0 copy-start.5
  73.9 1.4 %copy-done.5 = f32[1024,384]{1,0:T(8,128)S(1)} copy-done((f32[1024,384]{1,0:T(8,128)S(1)}, f32[1024,384]{1,0:T(8,128)}, u32[]{:S(2)}) %copy-start.5) | copy-done | bytes 1572888
  75.3 1.6 %shard_map.98 = f32[1024,384]{1,0:T(8,128)S(1)} custom-call(f32[1024,384]{1,0:T(8,128)S(1)} %bitcast.9, f32[1024,384]{1,0:T(8,128)S(1)} %copy-done.5, f32[1024,384]{1,0:T(8,128)} %copy-done.6), custom_call_target="tpu_custom_call" | custom-call | tf_op jit(solution)/shard_map/pallas_call | solution.py:296
  76.9 0.0 copy-start.1
  76.9 1.1 copy-done.1
  78.1 0.0 copy-start.12
  78.1 3.5 %all-to-all-start.2 = ((f32[32,32,384]{2,1,0:T(8,128)}), f32[32,32,384]{2,1,0:T(8,128)}, u32[]{:S(2)}, u32[]{:S(2)}) async-start(f32[32,32,384]{2,1,0:T(8,128)} %bitcast.11), calls=%async_computation.2 | async-start | bytes 3145728 | tf_op jit(solution)/shard_map/all_to_all | solution.py:242
  81.6 0.1 broadcast_in_dim_reshape.7.tiles
  81.7 0.0 copy-done.12
  81.7 0.1 copy.44
  81.8 0.1 reshape.67.pairs
  81.9 0.0 copy-start.7
  81.9 13.9 %shard_map.100.acc = f32[512,8,128]{2,1,0:T(8,128)S(1)} custom-call(s32[256]{0:T(256)S(1)} %reshape.67.pairs, f32[512,3,128]{2,1,0:T(4,128)S(1)} %copy.42.particles, s32[128,128,128]{2,1,0:T(8,128)} %contact.1), custom_call_target="tpu_custom_call" | custom-call | flops 67108864 | bytes 25165824 | tf_op jit(solution)/shard_map/pallas_call | solution.py:304
  95.8 0.0 copy-start
  95.9 1.3 %copy-done = f32[512,8,128]{2,1,0:T(8,128)} copy-done((f32[512,8,128]{2,1,0:T(8,128)}, f32[512,8,128]{2,1,0:T(8,128)S(1)}, u32[]{:S(2)}) %copy-start) | copy-done | bytes 2097176
  97.2 0.0 copy-done.7
  97.2 5.5 %shard_map.101 = f32[512,3,128]{2,1,0:T(4,128)S(1)} custom-call(f32[1024,384]{1,0:T(8,128)S(1)} %bitcast.10, s32[512,1]{1,0:T(8,128)S(1)} %copy-done.7, s32[512,128]{1,0:T(8,128)S(1)} %copy-done.2, f32[512,3,128]{2,1,0:T(4,128)S(1)} %copy.42.particles, f32[512,2,128]{2,1,0:T(2,128)S(1)} %copy-done.3, f32[512,8,128]{2,1,0:T(8,128)} %copy-done), custom_call_target="tpu_custom_call" | custom-call | flops 805306368 | bytes 10000000 | tf_op jit(solution)/shard_map/pallas_call | solution.py:321
  102.7 0.0 copy-start.10
  102.8 0.9 copy.47
  103.7 15.0 %all-to-all-done.2 = f32[32,32,384]{2,1,0:T(8,128)} async-done(((f32[32,32,384]{2,1,0:T(8,128)}), f32[32,32,384]{2,1,0:T(8,128)}, u32[]{:S(2)}, u32[]{:S(2)}) %all-to-all-start.2) | async-done | bytes 1572896 | tf_op jit(solution)/shard_map/all_to_all | solution.py:242
  118.7 0.0 copy-done.10
  118.7 4.1 %shard_map.99 = f32[3,64,1024]{2,1,0:T(8,128)} custom-call(f32[1024,384]{1,0:T(8,128)} %bitcast.5.got, s32[1,1024]{1,0:T(1,128)S(1)} %broadcast_in_dim_reshape.7.tiles, f32[3,64,1024]{2,1,0:T(8,128)S(1)} %copy-done.10), custom_call_target="tpu_custom_call" | custom-call | tf_op jit(solution)/shard_map/pallas_call | solution.py:327
  (1 shorter events, 0.0 us)
Async XLA Ops:
  0.6 12.7 %copy-start.8 = (f32[3,64,1024]{2,1,0:T(8,128)S(1)}, f32[3,64,1024]{2,1,0:T(8,128)}, u32[]{:S(2)}) copy-start(f32[3,64,1024]{2,1,0:T(8,128)} %gas.1) | copy-start | bytes 2359300
  4.4 22.1 %all-to-all-start = ((s32[32,1,32]{2,1,0:T(1,128)}), s32[32,1,32]{2,1,0:T(1,128)S(1)}, u32[]{:S(2)}, u32[]{:S(2)}) async-start(s32[32,1,32]{2,1,0:T(1,128)} %all_to_all.20), calls=%async_computation | async-start | bytes 32768 | tf_op jit(solution)/shard_map/all_to_all | solution.py:242
  13.3 1.0 copy-start.11
  25.6 0.9 copy-start.9
  31.4 6.9 %copy-start.2 = (s32[512,128]{1,0:T(8,128)S(1)}, s32[512,128]{1,0:T(8,128)}, u32[]{:S(2)}) copy-start(s32[512,128]{1,0:T(8,128)} %cells.3) | copy-start | bytes 786436
  31.4 6.9 %copy-start.3 = (f32[512,2,128]{2,1,0:T(2,128)S(1)}, f32[512,2,128]{2,1,0:T(2,128)}, u32[]{:S(2)}) copy-start(f32[512,2,128]{2,1,0:T(2,128)} %rates.3) | copy-start | bytes 1572868
  31.4 42.5 %all-to-all-start.1 = ((f32[32,32,384]{2,1,0:T(8,128)}), f32[32,32,384]{2,1,0:T(8,128)S(1)}, u32[]{:S(2)}, u32[]{:S(2)}) async-start(f32[32,32,384]{2,1,0:T(8,128)} %bitcast.2), calls=%async_computation.1 | async-start | bytes 3145728 | tf_op jit(solution)/shard_map/all_to_all | solution.py:242
  62.4 1.2 copy-start.4
  63.5 1.2 copy-start.6
  73.9 1.4 %copy-start.5 = (f32[1024,384]{1,0:T(8,128)S(1)}, f32[1024,384]{1,0:T(8,128)}, u32[]{:S(2)}) copy-start(f32[1024,384]{1,0:T(8,128)} %copy-done.4) | copy-start | bytes 4718596
  76.9 1.1 copy-start.1
  78.1 3.6 %copy-start.12 = (s32[128,2]{0,1:T(2,128)S(1)}, s32[128,2]{0,1:T(2,128)}, u32[]{:S(2)}) copy-start(s32[128,2]{0,1:T(2,128)} %param.14) | copy-start | bytes 3076
  78.1 40.6 %all-to-all-start.2 = ((f32[32,32,384]{2,1,0:T(8,128)}), f32[32,32,384]{2,1,0:T(8,128)}, u32[]{:S(2)}, u32[]{:S(2)}) async-start(f32[32,32,384]{2,1,0:T(8,128)} %bitcast.11), calls=%async_computation.2 | async-start | bytes 3145728 | tf_op jit(solution)/shard_map/all_to_all | solution.py:242
  81.9 15.3 %copy-start.7 = (s32[512,1]{1,0:T(8,128)S(1)}, s32[512,1]{1,0:T(8,128)}, u32[]{:S(2)}) copy-start(s32[512,1]{1,0:T(8,128)} %get-tuple-element.28.slot_col) | copy-start | bytes 6148
  95.8 1.3 %copy-start = (f32[512,8,128]{2,1,0:T(8,128)}, f32[512,8,128]{2,1,0:T(8,128)S(1)}, u32[]{:S(2)}) copy-start(f32[512,8,128]{2,1,0:T(8,128)S(1)} %shard_map.100.acc) | copy-start | bytes 6291460
  102.7 15.9 %copy-start.10 = (f32[3,64,1024]{2,1,0:T(8,128)S(1)}, f32[3,64,1024]{2,1,0:T(8,128)}, u32[]{:S(2)}) copy-start(f32[3,64,1024]{2,1,0:T(8,128)} %copy-done.9) | copy-start | bytes 2359300

commit v5 on v4

--- a/solution.py
+++ b/solution.py
@@ -28,7 +28,9 @@
 
 def select_rows(one_hot, values):
     high, low = split(values)
-    return dot(one_hot, high) + dot(one_hot, low)
+    width = values.shape[1]
+    both = dot(one_hot, jnp.concatenate([high, low], axis=1))
+    return both[:, :width] + both[:, width:]
 
 
 def tendency(v, xlo, xhi, wlo, whi, drift_x, drift_w):

time: 124 us -> 122 us (0.984)
  Pallas kernels: 63.6 us -> 60.8 us
  transfers between devices with their start and end apart: 3 -> 3, of which waited for: 2 -> 2; matrix products, arithmetic and copies ran while one was open for 4% -> 4% of each run, Pallas kernels for 45% -> 44%
where the time goes in v5:
time: 122 us; the launch traced here: 121 us
  Pallas kernels  60.8 us (50%)
  waiting for transfers between devices  25.4 us (21%)
  starting transfers between devices  15.8 us (13%)
  local copies, waits for them, and re-layouts  14.9 us (12%)
  other arithmetic  3.49 us (3%)
    all_to_all x3, waiting for transfers between devices, exchange(): lax.all_to_all(x, ('slab', 'pblk'), split_axis=0, concat_axis=0, tiled=True)  25.4 us
    pallas_call x1, Pallas kernels, on_device(): pl.pallas_call(sums_kernel, out_shape=(wide, wide), scratch_shapes=[pltpu...  23.8 us
    all_to_all x3, starting transfers between devices, exchange(): lax.all_to_all(x, ('slab', 'pblk'), split_axis=0, concat_axis=0, tiled=True)  15.8 us
    pallas_call x1, Pallas kernels, on_device(): pl.pallas_call(contact_kernel, grid_spec=pltpu.PrefetchScalarGridSpec(num...  13.9 us
    unnamed x29, local copies, waits for them, and re-layouts  11.6 us
    pallas_call x1, Pallas kernels, on_device(): pl.pallas_call(transport_kernel, out_shape=(field, jax.ShapeDtypeStruct((...  11.3 us
    pallas_call x1, Pallas kernels, on_device(): pl.pallas_call(particles_kernel, out_shape=jax.ShapeDtypeStruct(particles...  4.67 us
    pallas_call x1, Pallas kernels, on_device(): pl.pallas_call(sources_kernel, out_shape=field, scratch_shapes=[pltpu.VME...  3.35 us
  transfers between devices with their start and end apart: 3, of which 2 were waited for; matrix products, arithmetic and copies ran while one was open for 4% of the time, Pallas kernels for 44%

profile of v5, /device:TPU:1, one launch (start us, length us, event | category | flops | bytes accessed | tf_op | source)
XLA Modules:
  0.0 121.2 jit_solution(770985483769882933)
XLA Ops:
  0.6 0.0 copy-start.8
  0.6 1.0 convert_reduce_fusion
  1.7 1.1 slice_reduce_fusion
  2.8 0.7 add_select_fusion
  3.5 0.3 select_reduce_fusion
  3.7 0.7 all_to_all.20
  4.4 7.1 %all-to-all-start = ((s32[32,1,32]{2,1,0:T(1,128)}), s32[32,1,32]{2,1,0:T(1,128)S(1)}, u32[]{:S(2)}, u32[]{:S(2)}) async-start(s32[32,1,32]{2,1,0:T(1,128)} %all_to_all.20), calls=%async_computation | async-start | bytes 32768 | tf_op jit(solution)/shard_map/all_to_all | solution.py:244
  11.5 0.8 copy.39
  12.4 0.1 copy.43
  12.5 0.7 multiply_add_fusion
  13.3 0.0 copy-done.8
  13.3 0.0 copy-start.11
  13.3 1.0 copy-done.11
  14.3 11.3 %shard_map.95 = (f32[3,64,1024]{2,1,0:T(8,128)S(1)}, f32[3,512,128]{2,1,0:T(8,128)S(1)}) custom-call(f32[3,64,1024]{2,1,0:T(8,128)S(1)} %copy-done.8, f32[2,64,1024]{2,1,0:T(8,128)S(1)} %copy-done.11), custom_call_target="tpu_custom_call" | custom-call | flops 7864320 | bytes 30000000 | tf_op jit(solution)/shard_map/pallas_call | solution.py:267
  25.6 0.0 copy-start.9
  25.6 0.9 copy-done.9
  26.5 0.0 all-to-all-done
  26.5 0.6 broadcast.52
  27.1 0.7 reduce.9
  27.8 0.5 broadcast_in_dim_reshape.8.tiles
  28.3 2.2 %shard_map.96 = f32[1024,384]{1,0:T(8,128)} custom-call(f32[3,512,128]{2,1,0:T(8,128)S(1)} %get-tuple-element.10.table, s32[1024,1]{1,0:T(8,128)S(1)} %broadcast_in_dim_reshape.8.tiles), custom_call_target="tpu_custom_call" | custom-call | tf_op jit(solution)/shard_map/pallas_call | solution.py:286
  30.5 0.0 copy-start.2
  30.5 0.0 copy-start.3
  30.5 5.2 %all-to-all-start.1 = ((f32[32,32,384]{2,1,0:T(8,128)}), f32[32,32,384]{2,1,0:T(8,128)S(1)}, u32[]{:S(2)}, u32[]{:S(2)}) async-start(f32[32,32,384]{2,1,0:T(8,128)} %bitcast.2), calls=%async_computation.1 | async-start | bytes 3145728 | tf_op jit(solution)/shard_map/all_to_all | solution.py:244
  35.7 1.7 %copy.42.particles = f32[512,3,128]{2,1,0:T(4,128)S(1)} copy(f32[512,3,128]{2,0,1:T(8,128)} %param.10) | data formatting | bytes 1572864 | tf_op args[2]
  37.4 0.0 copy-done.2
  37.4 0.0 copy-done.3
  37.4 23.8 %shard_map.97 = (f32[1024,384]{1,0:T(8,128)S(1)}, f32[1024,384]{1,0:T(8,128)S(1)}) custom-call(s32[1,512]{1,0:T(1,128)S(1)} %add.21.slot_row, s32[512,128]{1,0:T(8,128)S(1)} %copy-done.2, f32[512,3,128]{2,1,0:T(4,128)S(1)} %copy.42.particles, f32[512,2,128]{2,1,0:T(2,128)S(1)} %copy-done.3), custom_call_target="tpu_custom_call" | custom-call | flops 268435456 | bytes 80000000 | tf_op jit(solution)/shard_map/pallas_call | solution.py:290
  61.2 0.0 copy-start.4
  61.2 1.1 copy-done.4
  62.4 0.0 copy-start.6
  62.4 1.2 copy-done.6
  63.5 9.5 %all-to-all-done.1 = f32[32,32,384]{2,1,0:T(8,128)S(1)} async-done(((f32[32,32,384]{2,1,0:T(8,128)}), f32[32,32,384]{2,1,0:T(8,128)S(1)}, u32[]{:S(2)}, u32[]{:S(2)}) %all-to-all-start.1) | async-done | bytes 1572896 | tf_op jit(solution)/shard_map/all_to_all | solution.py:244
  73.1 0.0 copy-start.5
  73.1 1.4 %copy-done.5 = f32[1024,384]{1,0:T(8,128)S(1)} copy-done((f32[1024,384]{1,0:T(8,128)S(1)}, f32[1024,384]{1,0:T(8,128)}, u32[]{:S(2)}) %copy-start.5) | copy-done | bytes 1572888
  74.5 1.6 %shard_map.98 = f32[1024,384]{1,0:T(8,128)S(1)} custom-call(f32[1024,384]{1,0:T(8,128)S(1)} %bitcast.9, f32[1024,384]{1,0:T(8,128)S(1)} %copy-done.5, f32[1024,384]{1,0:T(8,128)} %copy-done.6), custom_call_target="tpu_custom_call" | custom-call | tf_op jit(solution)/shard_map/pallas_call | solution.py:298
  76.1 0.0 copy-start.1
  76.1 1.1 copy-done.1
  77.2 0.0 copy-start.12
  77.2 3.5 %all-to-all-start.2 = ((f32[32,32,384]{2,1,0:T(8,128)}), f32[32,32,384]{2,1,0:T(8,128)}, u32[]{:S(2)}, u32[]{:S(2)}) async-start(f32[32,32,384]{2,1,0:T(8,128)} %bitcast.11), calls=%async_computation.2 | async-start | bytes 3145728 | tf_op jit(solution)/shard_map/all_to_all | solution.py:244
  80.8 0.1 broadcast_in_dim_reshape.7.tiles
  80.8 0.0 copy-done.12
  80.8 0.1 copy.44
  81.0 0.1 reshape.67.pairs
  81.1 0.0 copy-start.7
  81.1 13.9 %shard_map.100.acc = f32[512,8,128]{2,1,0:T(8,128)S(1)} custom-call(s32[256]{0:T(256)S(1)} %reshape.67.pairs, f32[512,3,128]{2,1,0:T(4,128)S(1)} %copy.42.particles, s32[128,128,128]{2,1,0:T(8,128)} %contact.1), custom_call_target="tpu_custom_call" | custom-call | flops 67108864 | bytes 25165824 | tf_op jit(solution)/shard_map/pallas_call | solution.py:306
  95.0 0.0 copy-start
  95.0 1.3 %copy-done = f32[512,8,128]{2,1,0:T(8,128)} copy-done((f32[512,8,128]{2,1,0:T(8,128)}, f32[512,8,128]{2,1,0:T(8,128)S(1)}, u32[]{:S(2)}) %copy-start) | copy-done | bytes 2097176
  96.4 0.0 copy-done.7
  96.4 4.7 %shard_map.101 = f32[512,3,128]{2,1,0:T(4,128)S(1)} custom-call(f32[1024,384]{1,0:T(8,128)S(1)} %bitcast.10, s32[512,1]{1,0:T(8,128)S(1)} %copy-done.7, s32[512,128]{1,0:T(8,128)S(1)} %copy-done.2, f32[512,3,128]{2,1,0:T(4,128)S(1)} %copy.42.particles, f32[512,2,128]{2,1,0:T(2,128)S(1)} %copy-done.3, f32[512,8,128]{2,1,0:T(8,128)} %copy-done), custom_call_target="tpu_custom_call" | custom-call | flops 805306368 | bytes 10000000 | tf_op jit(solution)/shard_map/pallas_call | solution.py:323
  101.1 0.0 copy-start.10
  101.1 0.9 copy.47
  102.0 15.9 %all-to-all-done.2 = f32[32,32,384]{2,1,0:T(8,128)} async-done(((f32[32,32,384]{2,1,0:T(8,128)}), f32[32,32,384]{2,1,0:T(8,128)}, u32[]{:S(2)}, u32[]{:S(2)}) %all-to-all-start.2) | async-done | bytes 1572896 | tf_op jit(solution)/shard_map/all_to_all | solution.py:244
  117.9 0.0 copy-done.10
  117.9 3.3 %shard_map.99 = f32[3,64,1024]{2,1,0:T(8,128)} custom-call(f32[1024,384]{1,0:T(8,128)} %bitcast.5.got, s32[1,1024]{1,0:T(1,128)S(1)} %broadcast_in_dim_reshape.7.tiles, f32[3,64,1024]{2,1,0:T(8,128)S(1)} %copy-done.10), custom_call_target="tpu_custom_call" | custom-call | tf_op jit(solution)/shard_map/pallas_call | solution.py:329
  (1 shorter events, 0.0 us)
Async XLA Ops:
  0.6 12.7 %copy-start.8 = (f32[3,64,1024]{2,1,0:T(8,128)S(1)}, f32[3,64,1024]{2,1,0:T(8,128)}, u32[]{:S(2)}) copy-start(f32[3,64,1024]{2,1,0:T(8,128)} %gas.1) | copy-start | bytes 2359300
  4.4 22.1 %all-to-all-start = ((s32[32,1,32]{2,1,0:T(1,128)}), s32[32,1,32]{2,1,0:T(1,128)S(1)}, u32[]{:S(2)}, u32[]{:S(2)}) async-start(s32[32,1,32]{2,1,0:T(1,128)} %all_to_all.20), calls=%async_computation | async-start | bytes 32768 | tf_op jit(solution)/shard_map/all_to_all | solution.py:244
  13.3 1.0 copy-start.11
  25.6 0.9 copy-start.9
  30.5 6.9 %copy-start.2 = (s32[512,128]{1,0:T(8,128)S(1)}, s32[512,128]{1,0:T(8,128)}, u32[]{:S(2)}) copy-start(s32[512,128]{1,0:T(8,128)} %cells.3) | copy-start | bytes 786436
  30.5 6.9 %copy-start.3 = (f32[512,2,128]{2,1,0:T(2,128)S(1)}, f32[512,2,128]{2,1,0:T(2,128)}, u32[]{:S(2)}) copy-start(f32[512,2,128]{2,1,0:T(2,128)} %rates.3) | copy-start | bytes 1572868
  30.5 42.5 %all-to-all-start.1 = ((f32[32,32,384]{2,1,0:T(8,128)}), f32[32,32,384]{2,1,0:T(8,128)S(1)}, u32[]{:S(2)}, u32[]{:S(2)}) async-start(f32[32,32,384]{2,1,0:T(8,128)} %bitcast.2), calls=%async_computation.1 | async-start | bytes 3145728 | tf_op jit(solution)/shard_map/all_to_all | solution.py:244
  61.2 1.2 copy-start.4
  62.4 1.2 copy-start.6
  73.1 1.4 %copy-start.5 = (f32[1024,384]{1,0:T(8,128)S(1)}, f32[1024,384]{1,0:T(8,128)}, u32[]{:S(2)}) copy-start(f32[1024,384]{1,0:T(8,128)} %copy-done.4) | copy-start | bytes 4718596
  76.1 1.1 copy-start.1
  77.2 3.6 %copy-start.12 = (s32[128,2]{0,1:T(2,128)S(1)}, s32[128,2]{0,1:T(2,128)}, u32[]{:S(2)}) copy-start(s32[128,2]{0,1:T(2,128)} %param.14) | copy-start | bytes 3076
  77.2 40.6 %all-to-all-start.2 = ((f32[32,32,384]{2,1,0:T(8,128)}), f32[32,32,384]{2,1,0:T(8,128)}, u32[]{:S(2)}, u32[]{:S(2)}) async-start(f32[32,32,384]{2,1,0:T(8,128)} %bitcast.11), calls=%async_computation.2 | async-start | bytes 3145728 | tf_op jit(solution)/shard_map/all_to_all | solution.py:244
  81.1 15.3 %copy-start.7 = (s32[512,1]{1,0:T(8,128)S(1)}, s32[512,1]{1,0:T(8,128)}, u32[]{:S(2)}) copy-start(s32[512,1]{1,0:T(8,128)} %get-tuple-element.28.slot_col) | copy-start | bytes 6148
  95.0 1.3 %copy-start = (f32[512,8,128]{2,1,0:T(8,128)}, f32[512,8,128]{2,1,0:T(8,128)S(1)}, u32[]{:S(2)}) copy-start(f32[512,8,128]{2,1,0:T(8,128)S(1)} %shard_map.100.acc) | copy-start | bytes 6291460
  101.1 16.8 %copy-start.10 = (f32[3,64,1024]{2,1,0:T(8,128)S(1)}, f32[3,64,1024]{2,1,0:T(8,128)}, u32[]{:S(2)}) copy-start(f32[3,64,1024]{2,1,0:T(8,128)} %copy-done.9) | copy-start | bytes 2359300

commit v6 on v5

--- a/solution.py
+++ b/solution.py
@@ -259,7 +259,9 @@
     asked = jnp.sum(
         jnp.where(slot[None, :] == jnp.arange(slots)[:, None], tile[None, :], 0), axis=1
     ).reshape(devices, depth)
-    tiles = exchange(asked).reshape(slots)
+    me = lax.axis_index("slab") * lax.axis_size("pblk") + lax.axis_index("pblk")
+    asked_all = lax.all_gather(asked, ("slab", "pblk"))
+    tiles = lax.dynamic_index_in_dim(asked_all, me, axis=1, keepdims=False).reshape(slots)
 
     field = jax.ShapeDtypeStruct(gas.shape, F32)
     wide = jax.ShapeDtypeStruct((slots, 3 * LANES), F32)

time: 122 us -> 185 us (1.52)
  blocking collectives: 0 us -> 68.4 us
  starting transfers between devices: 15.8 us -> 8.57 us
  Pallas kernels: 60.8 us -> 63.9 us
    all_gather x0 -> x1, blocking collectives: none -> 68.4 us  [on_device(): asked_all = lax.all_gather(asked, ('slab', 'pblk'))]
    all_to_all x3 -> x2, starting transfers between devices: 15.8 us -> 8.57 us  [exchange(): lax.all_to_all(x, ('slab', 'pblk'), split_axis=0, concat_axis=0, tiled=True)]
    pallas_call x1, Pallas kernels: 11.3 us -> 14.3 us  [on_device(): pl.pallas_call(transport_kernel, out_shape=(field, jax.ShapeDtypeStruct((...]
    all_to_all x3 -> x2, waiting for transfers between devices: 25.4 us -> 25.4 us  [exchange(): lax.all_to_all(x, ('slab', 'pblk'), split_axis=0, concat_axis=0, tiled=True)]
  transfers between devices with their start and end apart: 3 -> 2, of which waited for: 2 -> 2; matrix products, arithmetic and copies ran while one was open for 4% -> 2% of each run, Pallas kernels for 44% -> 23%
where the time goes in v6:
time: 185 us; the launch traced here: 184 us
  blocking collectives  68.4 us (37%)
  Pallas kernels  63.9 us (35%)
  waiting for transfers between devices  25.4 us (14%)
  local copies, waits for them, and re-layouts  14 us (8%)
  starting transfers between devices  8.57 us (5%)
  other arithmetic  2.75 us (1%)
    all_gather x1, blocking collectives, on_device(): asked_all = lax.all_gather(asked, ('slab', 'pblk'))  68.4 us
    all_to_all x2, waiting for transfers between devices, exchange(): lax.all_to_all(x, ('slab', 'pblk'), split_axis=0, concat_axis=0, tiled=True)  25.4 us
    pallas_call x1, Pallas kernels, on_device(): pl.pallas_call(sums_kernel, out_shape=(wide, wide), scratch_shapes=[pltpu...  23.8 us
    pallas_call x1, Pallas kernels, on_device(): pl.pallas_call(transport_kernel, out_shape=(field, jax.ShapeDtypeStruct((...  14.3 us
    pallas_call x1, Pallas kernels, on_device(): pl.pallas_call(contact_kernel, grid_spec=pltpu.PrefetchScalarGridSpec(num...  13.9 us
    unnamed x29, local copies, waits for them, and re-layouts  10.6 us
    all_to_all x2, starting transfers between devices, exchange(): lax.all_to_all(x, ('slab', 'pblk'), split_axis=0, concat_axis=0, tiled=True)  8.57 us
    pallas_call x1, Pallas kernels, on_device(): pl.pallas_call(particles_kernel, out_shape=jax.ShapeDtypeStruct(particles...  4.68 us
  transfers between devices with their start and end apart: 2, of which 2 were waited for; matrix products, arithmetic and copies ran while one was open for 2% of the time, Pallas kernels for 23%

profile of v6, /device:TPU:1, one launch (start us, length us, event | category | flops | bytes accessed | tf_op | source)
XLA Modules:
  0.0 183.8 jit_solution(11802829451736729008)
XLA Ops:
  0.6 0.0 copy-start.11
  0.6 0.0 copy-start.8
  0.7 0.9 copy.39
  1.6 1.0 convert_reduce_fusion
  2.6 1.1 slice_reduce_fusion
  3.7 0.7 add_select_fusion
  4.4 0.3 select_reduce_fusion
  4.7 0.1 all_gather_reshape.3
  4.8 0.1 copy.43
  4.9 68.4 %all_gather.3 = s32[32,32,32]{2,1,0:T(8,128)S(1)} all-gather(s32[1,32,32]{2,1,0:T(8,128)S(1)} %all_gather_reshape.3), channel_id=1, replica_groups=mesh['slab'=8,'pblk'=4] {'slab','pblk'}, dimensions={0}, use_global_device_ids=true | all-gather | bytes 135168 | tf_op jit(solution)/shard_map/all_gather | solution.py:263
  73.3 0.5 broadcast.52
  73.8 0.7 fusion.3
  74.5 0.5 broadcast_in_dim_reshape.8.tiles
  75.0 0.7 multiply_add_fusion
  75.8 0.0 copy-done.11
  75.8 0.0 copy-done.8
  75.8 14.3 %shard_map.95 = (f32[3,64,1024]{2,1,0:T(8,128)S(1)}, f32[3,512,128]{2,1,0:T(8,128)S(1)}) custom-call(f32[3,64,1024]{2,1,0:T(8,128)S(1)} %copy-done.8, f32[2,64,1024]{2,1,0:T(8,128)S(1)} %copy-done.11), custom_call_target="tpu_custom_call" | custom-call | flops 7864320 | bytes 30000000 | tf_op jit(solution)/shard_map/pallas_call | solution.py:269
  90.2 0.0 copy-start.9
  90.2 0.9 copy-done.9
  91.0 2.2 %shard_map.96 = f32[1024,384]{1,0:T(8,128)} custom-call(f32[3,512,128]{2,1,0:T(8,128)S(1)} %get-tuple-element.10.table, s32[1024,1]{1,0:T(8,128)S(1)} %broadcast_in_dim_reshape.8.tiles), custom_call_target="tpu_custom_call" | custom-call | tf_op jit(solution)/shard_map/pallas_call | solution.py:288
  93.2 0.0 copy-start.2
  93.2 0.0 copy-start.3
  93.2 5.1 %all-to-all-start = ((f32[32,32,384]{2,1,0:T(8,128)}), f32[32,32,384]{2,1,0:T(8,128)S(1)}, u32[]{:S(2)}, u32[]{:S(2)}) async-start(f32[32,32,384]{2,1,0:T(8,128)} %bitcast.2), calls=%async_computation | async-start | bytes 3145728 | tf_op jit(solution)/shard_map/all_to_all | solution.py:244
  98.3 1.7 copy.42.particles
  100.0 0.0 copy-done.2
  100.0 0.0 copy-done.3
  100.0 23.8 %shard_map.97 = (f32[1024,384]{1,0:T(8,128)S(1)}, f32[1024,384]{1,0:T(8,128)S(1)}) custom-call(s32[1,512]{1,0:T(1,128)S(1)} %add.28.slot_row, s32[512,128]{1,0:T(8,128)S(1)} %copy-done.2, f32[512,3,128]{2,1,0:T(4,128)S(1)} %copy.42.particles, f32[512,2,128]{2,1,0:T(2,128)S(1)} %copy-done.3), custom_call_target="tpu_custom_call" | custom-call | flops 268435456 | bytes 80000000 | tf_op jit(solution)/shard_map/pallas_call | solution.py:292
  123.8 0.0 copy-start.4
  123.8 1.1 copy-done.4
  124.9 0.0 copy-start.6
  124.9 1.1 copy-done.6
  126.1 9.6 %all-to-all-done = f32[32,32,384]{2,1,0:T(8,128)S(1)} async-done(((f32[32,32,384]{2,1,0:T(8,128)}), f32[32,32,384]{2,1,0:T(8,128)S(1)}, u32[]{:S(2)}, u32[]{:S(2)}) %all-to-all-start) | async-done | bytes 1572896 | tf_op jit(solution)/shard_map/all_to_all | solution.py:244
  135.6 0.0 copy-start.5
  135.6 1.4 copy-done.5
  137.1 1.6 shard_map.98
  138.7 0.0 copy-start.1
  138.7 1.1 copy-done.1
  139.8 0.0 copy-start.12
  139.8 3.5 %all-to-all-start.1 = ((f32[32,32,384]{2,1,0:T(8,128)}), f32[32,32,384]{2,1,0:T(8,128)}, u32[]{:S(2)}, u32[]{:S(2)}) async-start(f32[32,32,384]{2,1,0:T(8,128)} %bitcast.11), calls=%async_computation.1 | async-start | bytes 3145728 | tf_op jit(solution)/shard_map/all_to_all | solution.py:244
  143.4 0.1 broadcast_in_dim_reshape.7.tiles
  143.4 0.0 copy-done.12
  143.4 0.1 copy.44
  143.6 0.1 reshape.63.pairs
  143.7 0.0 copy-start.7
  143.7 13.9 %shard_map.100.acc = f32[512,8,128]{2,1,0:T(8,128)S(1)} custom-call(s32[256]{0:T(256)S(1)} %reshape.63.pairs, f32[512,3,128]{2,1,0:T(4,128)S(1)} %copy.42.particles, s32[128,128,128]{2,1,0:T(8,128)} %contact.1), custom_call_target="tpu_custom_call" | custom-call | flops 67108864 | bytes 25165824 | tf_op jit(solution)/shard_map/pallas_call | solution.py:308
  157.6 0.0 copy-start
  157.6 1.3 copy-done
  159.0 0.0 copy-done.7
  159.0 4.7 %shard_map.101 = f32[512,3,128]{2,1,0:T(4,128)S(1)} custom-call(f32[1024,384]{1,0:T(8,128)S(1)} %bitcast.10, s32[512,1]{1,0:T(8,128)S(1)} %copy-done.7, s32[512,128]{1,0:T(8,128)S(1)} %copy-done.2, f32[512,3,128]{2,1,0:T(4,128)S(1)} %copy.42.particles, f32[512,2,128]{2,1,0:T(2,128)S(1)} %copy-done.3, f32[512,8,128]{2,1,0:T(8,128)} %copy-done), custom_call_target="tpu_custom_call" | custom-call | flops 805306368 | bytes 10000000 | tf_op jit(solution)/shard_map/pallas_call | solution.py:325
  163.7 0.0 copy-start.10
  163.7 0.9 copy.47
  164.6 15.8 %all-to-all-done.1 = f32[32,32,384]{2,1,0:T(8,128)} async-done(((f32[32,32,384]{2,1,0:T(8,128)}), f32[32,32,384]{2,1,0:T(8,128)}, u32[]{:S(2)}, u32[]{:S(2)}) %all-to-all-start.1) | async-done | bytes 1572896 | tf_op jit(solution)/shard_map/all_to_all | solution.py:244
  180.5 0.0 copy-done.10
  180.5 3.3 %shard_map.99 = f32[3,64,1024]{2,1,0:T(8,128)} custom-call(f32[1024,384]{1,0:T(8,128)} %bitcast.5.got, s32[1,1024]{1,0:T(1,128)S(1)} %broadcast_in_dim_reshape.7.tiles, f32[3,64,1024]{2,1,0:T(8,128)S(1)} %copy-done.10), custom_call_target="tpu_custom_call" | custom-call | tf_op jit(solution)/shard_map/pallas_call | solution.py:331
  (1 shorter events, 0.0 us)
Async XLA Ops:
  0.6 75.2 %copy-start.11 = (f32[2,64,1024]{2,1,0:T(8,128)S(1)}, f32[2,64,1024]{2,1,0:T(8,128)}, u32[]{:S(2)}) copy-start(f32[2,64,1024]{2,1,0:T(8,128)} %drift.1) | copy-start | bytes 1572868
  0.6 75.2 %copy-start.8 = (f32[3,64,1024]{2,1,0:T(8,128)S(1)}, f32[3,64,1024]{2,1,0:T(8,128)}, u32[]{:S(2)}) copy-start(f32[3,64,1024]{2,1,0:T(8,128)} %gas.1) | copy-start | bytes 2359300
  90.2 0.9 copy-start.9
  93.2 6.7 %copy-start.2 = (s32[512,128]{1,0:T(8,128)S(1)}, s32[512,128]{1,0:T(8,128)}, u32[]{:S(2)}) copy-start(s32[512,128]{1,0:T(8,128)} %cells.3) | copy-start | bytes 786436
  93.2 6.8 %copy-start.3 = (f32[512,2,128]{2,1,0:T(2,128)S(1)}, f32[512,2,128]{2,1,0:T(2,128)}, u32[]{:S(2)}) copy-start(f32[512,2,128]{2,1,0:T(2,128)} %rates.3) | copy-start | bytes 1572868
  93.2 42.4 %all-to-all-start = ((f32[32,32,384]{2,1,0:T(8,128)}), f32[32,32,384]{2,1,0:T(8,128)S(1)}, u32[]{:S(2)}, u32[]{:S(2)}) async-start(f32[32,32,384]{2,1,0:T(8,128)} %bitcast.2), calls=%async_computation | async-start | bytes 3145728 | tf_op jit(solution)/shard_map/all_to_all | solution.py:244
  123.8 1.2 copy-start.4
  124.9 1.1 copy-start.6
  135.6 1.4 copy-start.5
  138.7 1.1 copy-start.1
  139.8 3.6 %copy-start.12 = (s32[128,2]{0,1:T(2,128)S(1)}, s32[128,2]{0,1:T(2,128)}, u32[]{:S(2)}) copy-start(s32[128,2]{0,1:T(2,128)} %param.14) | copy-start | bytes 3076
  139.8 40.6 %all-to-all-start.1 = ((f32[32,32,384]{2,1,0:T(8,128)}), f32[32,32,384]{2,1,0:T(8,128)}, u32[]{:S(2)}, u32[]{:S(2)}) async-start(f32[32,32,384]{2,1,0:T(8,128)} %bitcast.11), calls=%async_computation.1 | async-start | bytes 3145728 | tf_op jit(solution)/shard_map/all_to_all | solution.py:244
  143.7 15.3 %copy-start.7 = (s32[512,1]{1,0:T(8,128)S(1)}, s32[512,1]{1,0:T(8,128)}, u32[]{:S(2)}) copy-start(s32[512,1]{1,0:T(8,128)} %get-tuple-element.30.slot_col) | copy-start | bytes 6148
  157.6 1.3 copy-start
  163.7 16.8 %copy-start.10 = (f32[3,64,1024]{2,1,0:T(8,128)S(1)}, f32[3,64,1024]{2,1,0:T(8,128)}, u32[]{:S(2)}) copy-start(f32[3,64,1024]{2,1,0:T(8,128)} %copy-done.9) | copy-start | bytes 2359300
